TPU v7x, 128 devices: a whole 4x4x4 slice. The times are simulated.
128 devices in a mesh: rep: 8 (over y, core), neg: 16 (over x, z).
Axes of the slice: x: 4, y: 4, z: 4, core: 2. Of those that a mesh axis runs over, the one named last changes fastest.
Arguments:
- feature_table: bfloat16 [131072, 1024], P(('rep', 'neg')), may hold values from -6 to 6
- cur_rows: bfloat16 [98304, 1024], P(('rep', 'neg')), may hold values from -6 to 6
- next_owner: int32 [98304, 1], P(('rep', 'neg')), may hold values from 0 to 127; in each aligned block of 768 rows (0 to 767, 768 to 1535, ...) at most 12 rows name the same one
- next_local: int32 [98304], P(('rep', 'neg')), may hold values from 0 to 1023
- slot_counts: int32 [6144, 16], P(('rep', 'neg')), may hold values from 0 to 63, as said below
- hop_counts: int32 [512, 12], P(('rep', 'neg')), may hold values from 0 to 63, as said below
- positive_ids: int32 [512], P(('rep', 'neg')), may hold values from 0 to 1023
- neighbor_weight: bfloat16 [1024, 2048], replicated, may hold values from -0.1875 to 0.1875
- combine_weight: bfloat16 [3072, 2048], replicated, may hold values from -0.109375 to 0.109375
- candidates: bfloat16 [8192, 2048], P(('rep', 'neg')), may hold values from -0.296875 to 0.296875
Outputs:
- next_rows: bfloat16 [98304, 1024], P(('rep', 'neg'))
- query_loss: float32 [512], P(('rep', 'neg'))
- cand_grad: float32 [8192, 2048], P(('rep', 'neg'))
- neighbor_grad: float32 [1024, 2048], P(('rep', 'neg'))
Inputs may be any that keep to these rules, and one draw needn't show every extreme that they name: `next_owner`: among the 768 rows of one device no owner is named more than 12 times. `slot_counts`: 0 marks a padded slot; slot 0, the node itself, is at least 1. `hop_counts`: 0 marks a padded slot; the first is at least 1.
All inputs are finite; a program needn't handle non-finite values.
Results may differ from a plain program's by a relative error of at most 0.011.
The roundings to bfloat16 on the way count: a program that leaves them out, or rounds other values in their place, can miss the bound.
Values may be sent and summed in bfloat16 or wider, within the bound.
A program may use at most 128 MiB of HBM per device.

v0:
```python
import jax
import jax.numpy as jnp
from jax import lax
from jax.sharding import PartitionSpec as P

EPSILON = 1e-06
MARGIN = 0.5


def rms_scale(values):
    return values * lax.rsqrt(jnp.mean(values * values, axis=-1, keepdims=True) + EPSILON)


def local(
    feature_table,
    cur_rows,
    next_owner,
    next_local,
    slot_counts,
    hop_counts,
    positive_ids,
    neighbor_weight,
    combine_weight,
    candidates,
):
    devices = lax.axis_size(("rep", "neg"))
    request_count = cur_rows.shape[0]
    feature = cur_rows.shape[1]
    width = neighbor_weight.shape[1]
    hop_rows = slot_counts.shape[0]
    slot_count = slot_counts.shape[1]
    batch = hop_counts.shape[0]
    fanout = hop_counts.shape[1]
    capacity = 2 * request_count // devices
    owner_ids = next_owner[:, 0]
    owner_hits = (owner_ids[:, None] == jnp.arange(devices, dtype=jnp.int32)[None, :]).astype(
        jnp.int32
    )
    slot_rank = jnp.sum((jnp.cumsum(owner_hits, axis=0) - 1) * owner_hits, axis=1)
    requests = jnp.full((devices, capacity), -1, jnp.int32).at[owner_ids, slot_rank].set(next_local)
    asked = lax.all_to_all(requests, ("rep", "neg"), split_axis=0, concat_axis=0, tiled=True)
    present = asked >= 0
    fetched = feature_table[jnp.maximum(asked, 0)]
    returned = lax.all_to_all(
        jnp.where(present[..., None], fetched, jnp.zeros_like(fetched)),
        ("rep", "neg"),
        split_axis=0,
        concat_axis=0,
        tiled=True,
    )
    next_rows = returned[owner_ids, slot_rank]
    cand_all = lax.all_gather(candidates, "neg", axis=0, tiled=True)
    cand_total = cand_all.shape[0]
    projected = jnp.dot(cur_rows, neighbor_weight, preferred_element_type=jnp.float32)
    activated = jnp.maximum(projected, 0.0)
    slot_weight = slot_counts.astype(jnp.float32) / jnp.sum(
        slot_counts, axis=1, keepdims=True
    ).astype(jnp.float32)
    pooled = jnp.sum(
        slot_weight[:, :, None] * activated.reshape(hop_rows, slot_count, width), axis=1
    )
    pooled_low = pooled.astype(jnp.bfloat16)
    self_rows = cur_rows.reshape(hop_rows, slot_count, feature)[:, 0, :]
    mixed_in = jnp.dot(self_rows, combine_weight[:feature], preferred_element_type=jnp.float32)
    mixed_in = mixed_in + jnp.dot(
        pooled_low, combine_weight[feature:], preferred_element_type=jnp.float32
    )
    mixed = jnp.maximum(mixed_in, 0.0)
    normed = rms_scale(mixed)
    hop_weight = hop_counts.astype(jnp.float32) / jnp.sum(hop_counts, axis=1, keepdims=True).astype(
        jnp.float32
    )
    top_in = jnp.sum(hop_weight[:, :, None] * normed.reshape(batch, fanout, width), axis=1)
    embedding = rms_scale(top_in).astype(jnp.bfloat16)
    scores = lax.dot_general(
        embedding, cand_all, (((1,), (1,)), ((), ())), preferred_element_type=jnp.float32
    )
    positive_score = jnp.take_along_axis(scores, positive_ids[:, None], axis=1)
    gaps = scores - positive_score + MARGIN
    query_loss = jnp.mean(jax.nn.softplus(gaps), axis=1)
    sigmoid_gaps = jax.nn.sigmoid(gaps)
    totals = jnp.sum(sigmoid_gaps, axis=1, keepdims=True)
    chosen = jnp.arange(cand_total, dtype=jnp.int32)[None, :] == positive_ids[:, None]
    score_grad = ((sigmoid_gaps - jnp.where(chosen, totals, 0.0)) / cand_total).astype(jnp.bfloat16)
    cand_grad = lax.psum_scatter(
        lax.dot_general(
            score_grad, embedding, (((0,), (0,)), ((), ())), preferred_element_type=jnp.float32
        ),
        "neg",
        scatter_dimension=0,
        tiled=True,
    )
    embed_grad = jnp.dot(score_grad, cand_all, preferred_element_type=jnp.float32)
    unused_top, top_back = jax.vjp(rms_scale, top_in)
    top_grad = top_back(embed_grad)[0]
    normed_grad = (hop_weight[:, :, None] * top_grad[:, None, :]).reshape(hop_rows, width)
    unused_mid, mid_back = jax.vjp(rms_scale, mixed)
    mixed_grad = mid_back(normed_grad)[0]
    mixed_in_grad = jnp.where(mixed_in > 0.0, mixed_grad, 0.0).astype(jnp.bfloat16)
    pooled_grad = lax.dot_general(
        mixed_in_grad,
        combine_weight[feature:],
        (((1,), (1,)), ((), ())),
        preferred_element_type=jnp.float32,
    )
    activated_grad = (slot_weight[:, :, None] * pooled_grad[:, None, :]).reshape(
        request_count, width
    )
    projected_grad = jnp.where(projected > 0.0, activated_grad, 0.0).astype(jnp.bfloat16)
    neighbor_grad = lax.psum_scatter(
        lax.dot_general(
            cur_rows, projected_grad, (((0,), (0,)), ((), ())), preferred_element_type=jnp.float32
        ),
        ("rep", "neg"),
        scatter_dimension=0,
        tiled=True,
    )
    return (next_rows, query_loss, cand_grad, neighbor_grad)


def solution(mesh):
    return jax.shard_map(
        local,
        mesh=mesh,
        in_specs=(
            P(("rep", "neg"), None),
            P(("rep", "neg"), None),
            P(("rep", "neg"), None),
            P(("rep", "neg")),
            P(("rep", "neg"), None),
            P(("rep", "neg"), None),
            P(("rep", "neg")),
            P(),
            P(),
            P(("rep", "neg"), None),
        ),
        out_specs=(
            P(("rep", "neg"), None),
            P(("rep", "neg")),
            P(("rep", "neg"), None),
            P(("rep", "neg"), None),
        ),
        check_vma=False,
    )
```

profile of v0, /device:TPU:0, one launch (start us, length us, event | category | flops | bytes accessed | tf_op | source)
XLA Modules:
  0.0 878.6 jit_solution(2425783353266775084)
XLA Ops:
  7.2 0.0 copy-start
  7.2 0.0 all-gather.2.cloned.1.call-start
  7.2 0.7 all-gather.2.cloned.1.call-update
  7.9 0.0 reduce-scatter.7.cloned.1.call-start
  8.0 0.7 reduce_sum.120
  8.7 0.7 convert_divide_fusion
  9.4 0.1 copy.47
  9.5 1.3 slice.30
  10.7 0.1 mul.143
  10.8 8.8 broadcast_maximum_fusion
  19.6 1.8 multiply_reduce_fusion
  21.4 5.2 fusion.2
  26.5 0.0 copy-start.3
  26.6 0.0 copy-start.4
  26.6 3.2 multiply_reduce_fusion.3
  29.8 0.1 maximum_multiply_fusion
  29.9 0.0 copy-done.3
  29.9 0.1 reduce_sum.104
  30.1 0.1 convert_divide_fusion.1
  30.1 0.1 mul.145
  30.2 0.0 copy-done.4
  30.2 0.2 multiply_reduce_fusion.1
  30.4 0.1 multiply_reduce_fusion.5
  30.6 33.8 %all-gather.2.cloned.1.call-done = bf16[1024,2048]{1,0:T(8,128)(2,1)} async-done(((bf16[64,2048]{1,0:T(8,128)(2,1)}), bf16[1024,2048]{1,0:T(8,128)(2,1)}) %all-gather.2.cloned.1.call-update) | async-done | bytes 4194320 | tf_op jit(solution)/shard_map/all_gather | solution.py:52
  64.4 3.4 fusion.33
  67.7 0.7 gather_fusion.2
  68.4 0.2 fusion.35
  68.6 3.0 multiply_reduce_fusion.4
  71.6 0.1 add_add_fusion.2
  71.8 0.2 multiply_reduce_fusion.2
  72.1 6.0 fusion
  78.1 0.0 copy-start.1
  78.1 3.7 fusion.5
  81.8 0.0 copy-done.1
  81.8 5.8 convolution_bitcast_fusion
  87.7 9.1 %copy.50 = f32[1024,2048]{1,0:T(8,128)} copy(f32[1024,2048]{0,1:T(8,128)} %convolution_bitcast_fusion) | data formatting | bytes 16777216
  96.8 0.0 reduce-scatter.7.cloned.1.call-update
  96.8 0.0 reduce-scatter.5.cloned.1.call-start
  96.9 4.6 fusion.32
  101.5 0.0 reduce-scatter.5.cloned.1.call-update
  101.5 0.7 copy-done.2
  102.2 0.1 copy.39
  102.3 0.2 fusion.11
  102.5 0.1 add_add_fusion.1
  102.6 0.1 copy.40
  102.7 0.3 fusion.15
  103.0 0.0 copy-done.5
  103.0 36.6 %scatter_fusion = s32[128,12]{0,1:T(8,128)S(1)} fusion(s32[128,12]{0,1:T(8,128)S(1)} %broadcast_in_dim.24, s32[768]{0:T(1024)S(1)} %get-tuple-element.27, s32[768]{0:T(1024)S(1)} %copy-done.5), kind=kCustom, calls=%fused_computation.3 | custom fusion | bytes 15360 | tf_op jit(solution)/shard_map/scatter | solution.py:40
  139.6 0.1 copy.41
  139.8 17.5 %all_to_all.14 = s32[128,1,12]{2,1,0:T(1,128)S(1)} all-to-all(s32[128,1,12]{2,1,0:T(1,128)S(1)} %copy.41), channel_id=1, replica_groups=mesh['rep'=8,'neg'=16] {'rep','neg'}, dimensions={0} | all-to-all | bytes 12288 | tf_op jit(solution)/shard_map/all_to_all | solution.py:41
  157.3 0.1 copy.42
  157.4 0.1 copy.45
  157.5 0.1 reshape.155
  157.6 0.0 copy-done
  157.6 5.9 gather_fusion
  163.5 6.1 reshape.154
  169.6 0.1 copy.43
  169.7 2.5 broadcast_select_fusion
  172.2 58.4 %all_to_all.15 = bf16[128,12,1024]{2,1,0:T(8,128)(2,1)S(1)} all-to-all(bf16[128,12,1024]{2,1,0:T(8,128)(2,1)S(1)} %broadcast_select_fusion), channel_id=1, replica_groups=mesh['rep'=8,'neg'=16] {'rep','neg'}, dimensions={0} | all-to-all | bytes 6291456 | tf_op jit(solution)/shard_map/all_to_all | solution.py:44
  230.6 3.4 copy.46
  234.0 11.4 %gather_fusion.1 = bf16[768,1024]{1,0:T(8,128)(2,1)} fusion(bf16[128,12,1024]{2,0,1:T(8,128)(2,1)} %copy.46, s32[768]{0:T(1024)S(1)} %get-tuple-element.26), kind=kCustom, calls=%fused_computation.1 | custom fusion | bytes 3151872 | tf_op jit(solution)/shard_map/gather | solution.py:51
  245.4 0.5 broadcast_multiply_fusion
  245.9 542.6 %reduce-scatter.7.cloned.1.call-done = f32[8,2048]{1,0:T(8,128)} async-done(((f32[1024,2048]{1,0:T(8,128)}), f32[8,2048]{1,0:T(8,128)}) %reduce-scatter.7.cloned.1.call-update) | async-done | bytes 65552
  788.5 83.6 %reduce-scatter.5.cloned.1.call-done = f32[64,2048]{1,0:T(8,128)} async-done(((f32[1024,2048]{1,0:T(8,128)}), f32[64,2048]{1,0:T(8,128)}) %reduce-scatter.5.cloned.1.call-update) | async-done | bytes 524304 | tf_op jit(solution)/shard_map/reduce_scatter | solution.py:85
  (24 shorter events, 0.3 us)
Async XLA Ops:
  7.2 150.5 %copy-start = (bf16[1024,1024]{1,0:T(8,128)(2,1)S(1)}, bf16[1024,1024]{1,0:T(8,128)(2,1)}, u32[]{:S(2)}) copy-start(bf16[1024,1024]{1,0:T(8,128)(2,1)} %param.10) | copy-start | bytes 6291460
  7.2 57.2 %all-gather.2.cloned.1.call-start = ((), (), s32[]{:S(2)}) async-start(), calls=%async_computation.4 | async-start | bytes 4456448 | tf_op jit(solution)/shard_map/all_gather | solution.py:52
  7.9 780.6 %reduce-scatter.7.cloned.1.call-start = ((), (), s32[]{:S(2)}) async-start(), calls=%async_computation.6 | async-start | bytes 8454144
  26.5 3.4 copy-start.3
  26.6 3.7 copy-start.4
  78.1 3.7 copy-start.1
  96.8 775.2 %reduce-scatter.5.cloned.1.call-start = ((), (), s32[]{:S(2)}) async-start(), calls=%async_computation.5 | async-start | bytes 8912896 | tf_op jit(solution)/shard_map/reduce_scatter | solution.py:85
  101.5 0.7 copy-start.2
  101.5 1.5 copy-start.5
Sparse Core Ops, SparseCore 0:
  10.2 54.1 all-gather.1
  97.0 691.4 reduce-scatter.6
  792.8 79.1 reduce-scatter.4
where the time goes:
time: 878 us; the launch traced here: 879 us
  waiting for transfers between devices  661 us (75%)
  local copies, waits for them, and re-layouts  76.2 us (9%)
  blocking collectives  76 us (9%)
  matrix products  40 us (5%)
  between operations  14 us (2%)
  other arithmetic  11.7 us (1%)
    unnamed x4, waiting for transfers between devices  543 us
    reduce_scatter x1, waiting for transfers between devices, local(): lax.psum_scatter(lax.dot_general(score_grad, embedding, (((0,), (0,)), ((...  83.6 us
    all_to_all x1, blocking collectives, local(): lax.all_to_all(jnp.where(present[..., None], fetched, jnp.zeros_like(fetc...  58.4 us
    scatter x1, local copies, waits for them, and re-layouts, local(): jnp.full((devices, capacity), -1, jnp.int32).at[owner_ids, slot_rank]  36.6 us
    all_gather x1, waiting for transfers between devices, local(): cand_all = lax.all_gather(candidates, 'neg', axis=0, tiled=True)  33.8 us
  transfers between devices with their start and end apart: 3, of which 3 were waited for; matrix products, arithmetic and copies ran while one was open for 11% of the time, Pallas kernels for 0%

commit v1 on v0

--- a/solution.py
+++ b/solution.py
@@ -40,15 +40,15 @@
     requests = jnp.full((devices, capacity), -1, jnp.int32).at[owner_ids, slot_rank].set(next_local)
     asked = lax.all_to_all(requests, ("rep", "neg"), split_axis=0, concat_axis=0, tiled=True)
     present = asked >= 0
-    fetched = feature_table[jnp.maximum(asked, 0)]
+    fetched = feature_table.reshape(-1, 8, feature // 8)[jnp.maximum(asked, 0)]
     returned = lax.all_to_all(
-        jnp.where(present[..., None], fetched, jnp.zeros_like(fetched)),
+        jnp.where(present[..., None, None], fetched, jnp.zeros_like(fetched)),
         ("rep", "neg"),
         split_axis=0,
         concat_axis=0,
         tiled=True,
     )
-    next_rows = returned[owner_ids, slot_rank]
+    next_rows = returned[owner_ids, slot_rank].reshape(request_count, feature)
     cand_all = lax.all_gather(candidates, "neg", axis=0, tiled=True)
     cand_total = cand_all.shape[0]
     projected = jnp.dot(cur_rows, neighbor_weight, preferred_element_type=jnp.float32)
@@ -82,13 +82,15 @@
     totals = jnp.sum(sigmoid_gaps, axis=1, keepdims=True)
     chosen = jnp.arange(cand_total, dtype=jnp.int32)[None, :] == positive_ids[:, None]
     score_grad = ((sigmoid_gaps - jnp.where(chosen, totals, 0.0)) / cand_total).astype(jnp.bfloat16)
-    cand_grad = lax.psum_scatter(
-        lax.dot_general(
-            score_grad, embedding, (((0,), (0,)), ((), ())), preferred_element_type=jnp.float32
-        ),
-        "neg",
-        scatter_dimension=0,
-        tiled=True,
+    own = candidates.shape[0]
+    grad_split = score_grad.reshape(batch, cand_total // own, own)
+    grad_all = lax.all_to_all(grad_split, "neg", split_axis=1, concat_axis=0, tiled=True)
+    embed_all = lax.all_gather(embedding, "neg", axis=0, tiled=True)
+    cand_grad = lax.dot_general(
+        grad_all.reshape(cand_total // own * batch, own),
+        embed_all,
+        (((0,), (0,)), ((), ())),
+        preferred_element_type=jnp.float32,
     )
     embed_grad = jnp.dot(score_grad, cand_all, preferred_element_type=jnp.float32)
     unused_top, top_back = jax.vjp(rms_scale, top_in)
@@ -107,14 +109,15 @@
         request_count, width
     )
     projected_grad = jnp.where(projected > 0.0, activated_grad, 0.0).astype(jnp.bfloat16)
-    neighbor_grad = lax.psum_scatter(
-        lax.dot_general(
-            cur_rows, projected_grad, (((0,), (0,)), ((), ())), preferred_element_type=jnp.float32
-        ),
-        ("rep", "neg"),
-        scatter_dimension=0,
-        tiled=True,
+    partial = lax.dot_general(
+        cur_rows, projected_grad, (((0,), (0,)), ((), ())), preferred_element_type=jnp.float32
     )
+    reps, negs = lax.axis_size("rep"), lax.axis_size("neg")
+    partial = partial.reshape(reps, negs, feature // devices, width).swapaxes(0, 1)
+    partial = lax.psum_scatter(
+        partial.reshape(feature, width), "neg", scatter_dimension=0, tiled=True
+    )
+    neighbor_grad = lax.psum_scatter(partial, "rep", scatter_dimension=0, tiled=True)
     return (next_rows, query_loss, cand_grad, neighbor_grad)
 
 

time: 878 us -> 253 us (0.29)
  waiting for transfers between devices: 661 us -> 87.4 us
  blocking collectives: 76 us -> 24.1 us
  starting transfers between devices: 0.12 us -> 17.1 us
  local copies, waits for them, and re-layouts: 76.2 us -> 61.5 us
    unnamed x4 -> x3, waiting for transfers between devices: 543 us -> 0.71 us
    all_to_all x2 -> x0, blocking collectives: 76 us -> none  [the longest x1 58.4 us: local(): lax.all_to_all(jnp.where(present[..., None], fetched, jnp.zeros_like(fetc...]
    reduce_scatter x1 -> x2, waiting for transfers between devices: 83.6 us -> 40 us  [the longest x1 40 us: local(): lax.psum_scatter(partial.reshape(feature, width), 'neg', scatter_dimensio...]
    all_gather x0 -> x1, blocking collectives: none -> 24.1 us  [local(): embed_all = lax.all_gather(embedding, 'neg', axis=0, tiled=True)]
    all_to_all x0 -> x3, starting transfers between devices: none -> 17 us  [the longest x1 8.25 us: local(): lax.all_to_all(requests, ('rep', 'neg'), split_axis=0, concat_axis=0, til...]
    gather x3 -> x2, local copies, waits for them, and re-layouts: 23.3 us -> 9.88 us  [the longest x1 5 us: local(): fetched = feature_table.reshape(-1, 8, feature // 8)[jnp.maximum(asked, 0)]]
    all_to_all x0 -> x3, waiting for transfers between devices: none -> 12.9 us  [the longest x1 7.06 us: local(): lax.all_to_all(requests, ('rep', 'neg'), split_axis=0, concat_axis=0, til...]
  transfers between devices with their start and end apart: 3 -> 6, of which waited for: 3 -> 4; matrix products, arithmetic and copies ran while one was open for 11% -> 34% of each run, Pallas kernels for 0% -> 0%
where the time goes in v1:
time: 253 us; the launch traced here: 252 us
  waiting for transfers between devices  87.4 us (35%)
  local copies, waits for them, and re-layouts  61.5 us (24%)
  matrix products  34.6 us (14%)
  blocking collectives  24.1 us (10%)
  starting transfers between devices  17.1 us (7%)
  between operations  14.1 us (6%)
  other arithmetic  13.5 us (5%)
    reduce_scatter x1, waiting for transfers between devices, local(): lax.psum_scatter(partial.reshape(feature, width), 'neg', scatter_dimensio...  40 us
    scatter x1, local copies, waits for them, and re-layouts, local(): jnp.full((devices, capacity), -1, jnp.int32).at[owner_ids, slot_rank]  36.6 us
    all_gather x1, waiting for transfers between devices, local(): cand_all = lax.all_gather(candidates, 'neg', axis=0, tiled=True)  33.8 us
    all_gather x1, blocking collectives, local(): embed_all = lax.all_gather(embedding, 'neg', axis=0, tiled=True)  24.1 us
    dot_general x1, matrix products, local(): jnp.dot(cur_rows, neighbor_weight, preferred_element_type=jnp.float32)  8.76 us
    all_to_all x1, starting transfers between devices, local(): lax.all_to_all(requests, ('rep', 'neg'), split_axis=0, concat_axis=0, til...  8.25 us
    unnamed x20, local copies, waits for them, and re-layouts  7.49 us
    all_to_all x1, waiting for transfers between devices, local(): lax.all_to_all(requests, ('rep', 'neg'), split_axis=0, concat_axis=0, til...  7.06 us
  transfers between devices with their start and end apart: 6, of which 4 were waited for; matrix products, arithmetic and copies ran while one was open for 34% of the time, Pallas kernels for 0%

profile of v1, /device:TPU:0, one launch (start us, length us, event | category | flops | bytes accessed | tf_op | source)
XLA Modules:
  0.0 252.2 jit_solution(4715859251267090380)
XLA Ops:
  7.2 0.0 all-gather.3.cloned.1.call-start
  7.2 0.7 all-gather.3.cloned.1.call-update
  7.9 0.0 reduce-scatter.3.cloned.1.call-start
  7.9 0.7 reduce_sum.120
  8.7 0.7 convert_divide_fusion
  9.4 0.1 copy.48
  9.5 1.3 slice.30
  10.7 0.1 mul.143
  10.8 8.8 %broadcast_maximum_fusion = (f32[768,2048]{1,0:T(8,128)S(1)}, f32[768,2048]{1,0:T(8,128)}) fusion(bf16[768,1024]{1,0:T(8,128)(2,1)} %param.11, bf16[1024,2048]{1,0:T(8,128)(2,1)} %param.17), kind=kOutput, calls=%fused_computation.14 | convolution fusion | flops 3222798336 | bytes 18350080 | tf_op jit(solution)/shard_map/dot_general | solution.py:54
  19.5 1.8 multiply_reduce_fusion
  21.3 5.2 %fusion.2 = f32[48,2048]{1,0:T(8,128)S(1)} fusion(bf16[3072,2048]{1,0:T(8,128)(2,1)} %param.18, bf16[48,2048]{1,0:T(8,128)(2,1)S(1)} %multiply_reduce_fusion), kind=kOutput, calls=%fused_computation.6 | convolution fusion | flops 402653184 | bytes 8978432 | tf_op jit(solution)/shard_map/dot_general | solution.py:65
  26.5 3.2 %multiply_reduce_fusion.3 = (f32[48]{0:T(128)S(1)}, f32[48,2048]{1,0:T(8,128)S(1)}) fusion(f32[48,2048]{1,0:T(8,128)S(1)} %fusion.2, bf16[3072,2048]{1,0:T(8,128)(2,1)} %param.18, bf16[48,1,1024]{2,1,0:T(2,128)(2,1)S(1)} %slice.30), kind=kOutput, calls=%fused_computation.29 | convolution fusion | flops 201719760 | bytes 5079232 | tf_op jit(solution)/shard_map/dot_general | solution.py:64
  29.7 0.1 maximum_multiply_fusion
  29.9 0.1 reduce_sum.104
  30.0 0.1 convert_divide_fusion.1
  30.1 0.1 mul.145
  30.2 0.2 multiply_reduce_fusion.1
  30.4 0.1 multiply_reduce_fusion.5
  30.6 33.8 %all-gather.3.cloned.1.call-done = bf16[1024,2048]{1,0:T(8,128)(2,1)} async-done(((bf16[64,2048]{1,0:T(8,128)(2,1)}), bf16[1024,2048]{1,0:T(8,128)(2,1)}) %all-gather.3.cloned.1.call-update) | async-done | bytes 4194320 | tf_op jit(solution)/shard_map/all_gather | solution.py:52
  64.4 3.4 %fusion.33 = f32[4,1024]{1,0:T(4,128)S(1)} fusion(bf16[1024,2048]{1,0:T(8,128)(2,1)} %all-gather.3.cloned.1.call-done, f32[4,2048]{1,0:T(4,128)S(1)} %multiply_reduce_fusion.1, f32[4]{0:T(128)S(1)} %fusion.29), kind=kOutput, calls=%fused_computation.77 | convolution fusion | flops 16793600 | bytes 4243472 | tf_op jit(solution)/shard_map/dot_general | solution.py:75
  67.7 0.7 gather_fusion.2
  68.4 0.2 fusion.35
  68.6 0.1 multiply_convert_fusion.1
  68.7 3.0 %multiply_reduce_fusion.4 = (f32[4]{0:T(128)S(1)}, f32[4,2048]{1,0:T(4,128)S(1)}) fusion(f32[4,2048]{1,0:T(4,128)S(1)} %multiply_reduce_fusion.1, bf16[4,1024]{1,0:T(4,128)(2,1)S(1)} %multiply_convert_fusion.1, bf16[1024,2048]{1,0:T(8,128)(2,1)} %all-gather.3.cloned.1.call-done), kind=kOutput, calls=%fused_computation.42 | convolution fusion | flops 16793596 | bytes 4268048 | tf_op jit(solution)/shard_map/dot_general | solution.py:95
  71.7 0.1 add_add_fusion.2
  71.9 0.2 multiply_reduce_fusion.2
  72.1 6.2 %fusion = f32[48,2048]{1,0:T(8,128)S(1)} fusion(bf16[3072,2048]{1,0:T(8,128)(2,1)} %param.18, f32[48,2048]{1,0:T(8,128)S(1)} %get-tuple-element.14, f32[48,2048]{1,0:T(8,128)S(1)} %mul.153, f32[48]{0:T(128)S(1)} %multiply_multiply_fusion, f32[48]{0:T(128)S(1)} %mul.145, f32[48]{0:T(128)S(1)} %fusion.28), kind=kOutput, calls=%fused_computation.4 | convolution fusion | flops 403537920 | bytes 9568832 | tf_op jit(solution)/shard_map/dot_general | solution.py:102
  78.3 0.8 fusion.5
  79.1 0.6 copy-done
  79.7 3.9 %fusion.37 = f32[2048,1024]{0,1:T(8,128)S(1)} fusion(bf16[768,2048]{1,0:T(8,128)(2,1)S(1)} %fusion.5, bf16[768,1024]{1,0:T(8,128)(2,1)S(1)} %copy-done), kind=kOutput, calls=%fused_computation.82 | convolution fusion | flops 3221225472 | bytes 13107200 | tf_op jit(solution)/shard_map/dot_general | solution.py:112
  83.7 3.8 %copy.51 = f32[16,8,8,2048]{3,2,1,0:T(8,128)} copy(f32[16,8,8,2048]{3,2,0,1:T(8,128)S(1)} %bitcast.72) | data formatting | bytes 16777216 | tf_op jit(solution)/shard_map/transpose | solution.py:116
  87.5 0.0 reduce-scatter.3.cloned.1.call-update
  87.5 0.7 copy-done.1
  88.2 0.1 copy.41
  88.3 0.2 fusion.11
  88.5 0.1 add_add_fusion.1
  88.6 0.1 copy.42
  88.7 0.3 fusion.15
  89.0 36.6 %scatter_fusion = s32[128,12]{0,1:T(8,128)S(1)} fusion(s32[128,12]{0,1:T(8,128)S(1)} %broadcast_in_dim.24, s32[768]{0:T(1024)S(1)} %get-tuple-element.5, s32[768]{0:T(1024)S(1)} %copy-done.3), kind=kCustom, calls=%fused_computation.3 | custom fusion | bytes 15360 | tf_op jit(solution)/shard_map/scatter | solution.py:40
  125.6 0.7 copy.43
  126.4 8.3 %all-to-all-start = ((s32[128,1,12]{2,1,0:T(1,128)}), s32[128,1,12]{2,1,0:T(1,128)S(1)}, u32[]{:S(2)}, u32[]{:S(2)}) async-start(s32[128,1,12]{2,1,0:T(1,128)} %copy.43), calls=%async_computation | async-start | bytes 131072 | tf_op jit(solution)/shard_map/all_to_all | solution.py:41
  134.6 2.3 copy.53
  137.0 7.1 %all-to-all-done = s32[128,1,12]{2,1,0:T(1,128)S(1)} async-done(((s32[128,1,12]{2,1,0:T(1,128)}), s32[128,1,12]{2,1,0:T(1,128)S(1)}, u32[]{:S(2)}, u32[]{:S(2)}) %all-to-all-start) | async-done | bytes 6176 | tf_op jit(solution)/shard_map/all_to_all | solution.py:41
  144.1 0.1 copy.44
  144.1 0.1 copy.47
  144.3 0.1 reshape.180
  144.4 0.1 copy.45
  144.5 5.0 %gather_fusion = bf16[1536,8,128]{2,1,0:T(8,128)(2,1)} fusion(bf16[1024,8,128]{2,1,0:T(8,128)(2,1)S(1)} %bitcast.70, s32[2048]{0:T(1024)S(1)} %pad_clamp_fusion), kind=kCustom, calls=%fused_computation | custom fusion | bytes 6297600 | tf_op jit(solution)/shard_map/gather | solution.py:43
  149.5 7.0 %broadcast_select_fusion = bf16[128,12,8,128]{3,2,1,0:T(8,128)(2,1)} fusion(bf16[128,12,8,128]{3,2,1,0:T(8,128)(2,1)} %bitcast.71, pred[128,12]{1,0:T(8,128)(4,1)S(1)} %copy.45), kind=kLoop, calls=%fused_computation.15 | loop fusion | flops 1572864 | bytes 6292992 | tf_op jit(solution)/shard_map/jit(_where)/select_n | solution.py:45
  156.6 4.7 %all-to-all-start.1 = ((bf16[128,12,8,128]{3,2,1,0:T(8,128)(2,1)}), bf16[128,12,8,128]{3,2,1,0:T(8,128)(2,1)S(1)}, u32[]{:S(2)}, u32[]{:S(2)}) async-start(bf16[128,12,8,128]{3,2,1,0:T(8,128)(2,1)} %broadcast_select_fusion), calls=%async_computation.1 | async-start | bytes 6291456 | tf_op jit(solution)/shard_map/all_to_all | solution.py:44
  161.2 0.0 reduce-scatter.5.cloned.1.call-start
  161.3 40.0 %reduce-scatter.3.cloned.1.call-done = f32[64,2048]{1,0:T(8,128)} async-done(((f32[1024,2048]{1,0:T(8,128)}), f32[64,2048]{1,0:T(8,128)}) %reduce-scatter.3.cloned.1.call-update) | async-done | bytes 524304 | tf_op jit(solution)/shard_map/reduce_scatter | solution.py:117
  201.3 0.0 reduce-scatter.5.cloned.1.call-update
  201.3 5.8 %all-to-all-done.1 = bf16[128,12,8,128]{3,2,1,0:T(8,128)(2,1)S(1)} async-done(((bf16[128,12,8,128]{3,2,1,0:T(8,128)(2,1)}), bf16[128,12,8,128]{3,2,1,0:T(8,128)(2,1)S(1)}, u32[]{:S(2)}, u32[]{:S(2)}) %all-to-all-start.1) | async-done | bytes 3145760 | tf_op jit(solution)/shard_map/all_to_all | solution.py:44
  207.1 4.9 %gather_fusion.1 = bf16[768,8,128]{2,1,0:T(8,128)(2,1)} fusion(bf16[128,12,8,128]{3,2,1,0:T(8,128)(2,1)S(1)} %all-to-all-done.1, s32[768]{0:T(1024)S(1)} %get-tuple-element.4), kind=kCustom, calls=%fused_computation.1 | custom fusion | bytes 3151872 | tf_op jit(solution)/shard_map/gather | solution.py:51
  212.0 3.0 %copy.63 = bf16[96,8,8,128]{3,1,2,0:T(8,128)(2,1)} copy(bf16[96,8,8,128]{3,2,1,0:T(8,128)(2,1)} %bitcast.76) | data formatting | bytes 3145728
  215.0 0.1 reshape.174
  215.1 0.7 reshape.215
  215.8 4.0 %all-to-all-start.2 = ((bf16[16,2,128]{2,1,0:T(2,128)(2,1)}), bf16[16,2,128]{2,1,0:T(2,128)(2,1)S(1)}, u32[]{:S(2)}, u32[]{:S(2)}) async-start(bf16[16,2,128]{2,1,0:T(2,128)(2,1)} %reshape.215), calls=%async_computation.2 | async-start | bytes 16384 | tf_op jit(solution)/shard_map/all_to_all | solution.py:87
  219.8 0.5 broadcast_multiply_fusion
  220.4 24.1 %all-gather = bf16[16,4,2048]{2,1,0:T(4,128)(2,1)S(1)} all-gather(bf16[1,4,2048]{2,1,0:T(4,128)(2,1)S(1)} %get-tuple-element.9), channel_id=1, replica_groups=mesh['rep'=8,'neg'=16] {'neg'}, dimensions={0}, use_global_device_ids=true | all-gather | bytes 278528 | tf_op jit(solution)/shard_map/all_gather | solution.py:88
  244.5 0.1 reshape.210
  244.5 0.1 reshape.216
  244.6 1.0 fusion.36
  (38 shorter events, 0.4 us)
Async XLA Ops:
  7.2 57.2 %all-gather.3.cloned.1.call-start = ((), (), s32[]{:S(2)}) async-start(), calls=%async_computation.5 | async-start | bytes 4456448 | tf_op jit(solution)/shard_map/all_gather | solution.py:52
  7.9 193.4 %reduce-scatter.3.cloned.1.call-start = ((), (), s32[]{:S(2)}) async-start(), calls=%async_computation.6 | async-start | bytes 8912896 | tf_op jit(solution)/shard_map/reduce_scatter | solution.py:117
  26.5 3.4 %copy-start.2 = (s32[4,12]{1,0:T(4,128)S(1)}, s32[4,12]{1,0:T(4,128)}, u32[]{:S(2)}) copy-start(s32[4,12]{1,0:T(4,128)} %param.15) | copy-start | bytes 580
  26.5 3.7 %copy-start.4 = (s32[4]{0:T(128)S(1)}, s32[4]{0:T(128)}, u32[]{:S(2)}) copy-start(s32[4]{0:T(128)} %param.16) | copy-start | bytes 52
  71.8 6.5 %slice-start = ((s8[6291456]{0:T(1024)(128)(4,1)}), s8[2097152]{0:T(1024)(128)(4,1)S(1)}, s32[]{:S(2)}) async-start(s8[6291456]{0:T(1024)(128)(4,1)} %bitcast.73), calls=%async_computation.8 | async-start | bytes 4194304
  72.1 6.2 %slice-start.1 = ((s8[6291456]{0:T(1024)(128)(4,1)}), s8[4194304]{0:T(1024)(128)(4,1)S(1)}, s32[]{:S(2)}) async-start(s8[6291456]{0:T(1024)(128)(4,1)} %bitcast.73), calls=%async_computation.9 | async-start | bytes 8388608
  78.3 1.4 copy-start
  87.5 0.7 copy-start.1
  87.5 1.5 copy-start.3
  126.4 17.7 %all-to-all-start = ((s32[128,1,12]{2,1,0:T(1,128)}), s32[128,1,12]{2,1,0:T(1,128)S(1)}, u32[]{:S(2)}, u32[]{:S(2)}) async-start(s32[128,1,12]{2,1,0:T(1,128)} %copy.43), calls=%async_computation | async-start | bytes 131072 | tf_op jit(solution)/shard_map/all_to_all | solution.py:41
  156.6 50.5 %all-to-all-start.1 = ((bf16[128,12,8,128]{3,2,1,0:T(8,128)(2,1)}), bf16[128,12,8,128]{3,2,1,0:T(8,128)(2,1)S(1)}, u32[]{:S(2)}, u32[]{:S(2)}) async-start(bf16[128,12,8,128]{3,2,1,0:T(8,128)(2,1)} %broadcast_select_fusion), calls=%async_computation.1 | async-start | bytes 6291456 | tf_op jit(solution)/shard_map/all_to_all | solution.py:44
  161.2 84.4 %reduce-scatter.5.cloned.1.call-start = ((), (), s32[]{:S(2)}) async-start(), calls=%async_computation.7 | async-start | bytes 589824 | tf_op jit(solution)/shard_map/reduce_scatter | solution.py:120
  215.8 28.7 %all-to-all-start.2 = ((bf16[16,2,128]{2,1,0:T(2,128)(2,1)}), bf16[16,2,128]{2,1,0:T(2,128)(2,1)S(1)}, u32[]{:S(2)}, u32[]{:S(2)}) async-start(bf16[16,2,128]{2,1,0:T(2,128)(2,1)} %reshape.215), calls=%async_computation.2 | async-start | bytes 16384 | tf_op jit(solution)/shard_map/all_to_all | solution.py:87
Sparse Core Ops, SparseCore 0:
  10.1 54.1 all-gather.2
  87.6 113.6 reduce-scatter.2
  204.2 32.1 reduce-scatter.4

commit v2 on v0

v2 whole, which is shorter than its diff:
```python
import jax
import jax.numpy as jnp
from jax import lax
from jax.experimental import pallas as pl
from jax.experimental.pallas import tpu as pltpu
from jax.sharding import PartitionSpec as P

EPSILON = 1e-06
MARGIN = 0.5
MESH = pl.DeviceIdType.MESH
F32 = jnp.float32
BF16 = jnp.bfloat16
HIGH = lax.Precision.HIGHEST

REPS, NEGS, DEVS = 8, 16, 128
YS, CORES = 4, 2
F, H = 1024, 2048
TILE = 256
TILES = H // TILE
REQ, HOP1, SLOTS, B, K1 = 768, 48, 16, 4, 12
WIDE = 768
OWN = 64


def iota(shape, dim):
    return lax.broadcasted_iota(jnp.int32, shape, dim)


def nt(a, b, precision=None):
    return lax.dot_general(
        a, b, (((1,), (1,)), ((), ())), preferred_element_type=F32, precision=precision
    )


def tn(a, b, precision=None):
    return lax.dot_general(
        a, b, (((0,), (0,)), ((), ())), preferred_element_type=F32, precision=precision
    )


def nn(a, b, precision=None):
    return jnp.dot(a, b, preferred_element_type=F32, precision=precision)


def bf(mask):
    return mask.astype(F32).astype(BF16)


def kernel(
    owner_ref, local_ref, slot_ref, hop_ref, pos_ref,
    table_hbm, cur_hbm, nw_hbm, cw_hbm, cand_hbm,
    rows_hbm, loss_ref, cand_out, ngrad_ref,
    cur_v, curt_v, table_v, nw_v, cw_v, cand_v, mask_v, pgrad_v, x_v, mixed_v, pooled_g,
    req_send, req_recv, ids_v, row_send, row_recv, rows_acc, cols_v,
    emb_send, emb_all, e_v, sc_send, sc_all, eg_send, eg_recv,
    p_send, p_recv, p_own, a1_send, a1_recv, a2_f, a2_send, a2_recv,
    b1_f, b1_send, b1_recv, b2_f, b2_send, b2_recv,
    in_sem, out_sem, req_ssem, req_rsem, row_ssem, row_rsem,
    emb_ssem, emb_rsem, sc_ssem, sc_rsem, eg_ssem, eg_rsem,
    p_ssem, p_rsem, a1_ssem, a1_rsem, a2_ssem, a2_rsem, b1_ssem, b1_rsem, b2_ssem, b2_rsem,
):
    rep = lax.axis_index("rep")
    neg = lax.axis_index("neg")
    me = rep * NEGS + neg
    y, core = rep // CORES, rep % CORES

    loads = [
        pltpu.make_async_copy(cur_hbm, cur_v, in_sem.at[0]),
        pltpu.make_async_copy(table_hbm, table_v, in_sem.at[1]),
        pltpu.make_async_copy(cand_hbm, cand_v.at[pl.ds(0, OWN)], in_sem.at[2]),
        pltpu.make_async_copy(cand_hbm, cand_v.at[pl.ds(OWN, OWN)], in_sem.at[3]),
    ]
    nw_loads = [
        pltpu.make_async_copy(
            nw_hbm.at[:, pl.ds(j * TILE, TILE)], nw_v.at[j], in_sem.at[4 + j]
        )
        for j in range(TILES)
    ]
    cw_loads = [
        pltpu.make_async_copy(
            cw_hbm.at[:, pl.ds(j * TILE, TILE)], cw_v.at[j], in_sem.at[12 + j]
        )
        for j in range(TILES)
    ]
    loads[0].start()
    for load in nw_loads:
        load.start()
    for load in loads[1:]:
        load.start()
    for load in cw_loads:
        load.start()

    barrier = pltpu.get_barrier_semaphore()

    def greet(i, carry):
        d = lax.rem(me + i, DEVS)
        pl.semaphore_signal(
            barrier, inc=1, device_id=(d // NEGS, d % NEGS), device_id_type=MESH
        )
        return carry

    lax.fori_loop(1, DEVS, greet, 0)

    hit = owner_ref[...] == iota((DEVS, REQ), 0)
    hit_low = bf(hit)
    before = bf(iota((REQ, REQ), 0) < iota((REQ, REQ), 1))
    count = nn(hit_low, before)
    rank = jnp.sum(jnp.where(hit, count, 0.0), axis=0, keepdims=True)
    local = local_ref[...]
    line = iota((DEVS, REQ), 0).astype(F32)
    pay = jnp.where(line == rank, (local >> 5).astype(F32), 0.0) + jnp.where(
        line == rank + 16.0, (local & 31).astype(F32), 0.0
    )
    asks = nt(hit_low, pay.astype(BF16))
    lane1 = iota((1, 128), 1)
    positives = jnp.zeros((1, 128), jnp.int32)
    for t in range(B):
        value = pos_ref[0, t]
        positives = positives + jnp.where(lane1 == 32 + t, value >> 5, 0)
        positives = positives + jnp.where(lane1 == 36 + t, value & 31, 0)
    asks = asks + positives.astype(F32)
    req_send[...] = asks.reshape(DEVS, 1, 128)
    eye = bf(iota((REQ, REQ), 0) == iota((REQ, REQ), 1))
    pair = jnp.where(iota((16, REQ), 0) == 0, owner_ref[...].astype(F32), rank).astype(BF16)
    cols_v[...] = nt(eye, pair)

    pl.semaphore_wait(barrier, DEVS - 1)

    def ask(i, carry):
        d = lax.rem(me + i, DEVS)
        pltpu.make_async_remote_copy(
            src_ref=req_send.at[d],
            dst_ref=req_recv.at[me],
            send_sem=req_ssem.at[d],
            recv_sem=req_rsem.at[me],
            device_id=(d // NEGS, d % NEGS),
            device_id_type=MESH,
        ).start()
        return carry

    lax.fori_loop(1, DEVS, ask, 0)
    req_recv[me] = req_send[me]

    spread = bf(iota((REQ, HOP1), 0) // SLOTS == iota((REQ, HOP1), 1))
    counts = nt(spread, slot_ref[...].astype(F32).astype(BF16))
    at_slot = iota((REQ, SLOTS), 0) % SLOTS == iota((REQ, SLOTS), 1)
    weight = jnp.sum(jnp.where(at_slot, counts, 0.0), axis=1, keepdims=True) / jnp.sum(
        counts, axis=1, keepdims=True
    )

    loads[0].wait()
    for j in range(TILES):
        nw_loads[j].wait()
        projected = nn(cur_v[...], nw_v[j])
        mask_v[j] = bf(projected > 0.0)
        weighted = jnp.maximum(projected, 0.0) * weight
        pooled = jnp.sum(weighted.reshape(HOP1, SLOTS, TILE), axis=1)
        x_v[:, F + j * TILE : F + (j + 1) * TILE] = pooled.astype(BF16)
    first = bf(iota((HOP1, REQ), 0) * SLOTS == iota((HOP1, REQ), 1))
    x_v[:, 0:F] = nn(first, cur_v[...]).astype(BF16)

    def got_ask(i, carry):
        d = lax.rem(me + i, DEVS)
        pltpu.make_async_remote_copy(
            src_ref=req_send.at[d],
            dst_ref=req_recv.at[d],
            send_sem=req_ssem.at[d],
            recv_sem=req_rsem.at[d],
            device_id=(rep, neg),
            device_id_type=MESH,
        ).wait()
        return carry

    lax.fori_loop(1, DEVS, got_ask, 0)
    ids_v[...] = req_recv[...].reshape(DEVS, 128)
    loads[1].wait()

    def serve(step, carry):
        g = lax.rem(rep + step, REPS)
        base = pl.multiple_of(g * NEGS, NEGS)
        asked = ids_v[pl.ds(base, NEGS), :].astype(BF16)

        def chosen(rows, per, slot_of):
            wide = nn(bf(iota((rows, NEGS), 0) // per % NEGS == iota((rows, NEGS), 1)), asked)
            slot = slot_of(iota((rows, 1), 0))
            at = iota((rows, 128), 1)
            ids = jnp.sum(
                jnp.where(at == slot, wide * 32.0, 0.0) + jnp.where(at == slot + 16, wide, 0.0),
                axis=1,
                keepdims=True,
            )
            return bf(ids == iota((rows, F), 1).astype(F32))

        main = nn(chosen(256, 16, lambda r: r % 16), table_v[:, 0:WIDE]).reshape(NEGS, 16, WIDE)
        tail = nn(
            chosen(384, 8, lambda r: jnp.maximum(r % 8 - 4, 0) * 3 + r // 128),
            table_v[:, WIDE:F],
        )
        high = iota((NEGS, 8, TILE), 1) >= 4
        parts = []
        for c in range(3):
            own = main[:, 8:16, c * TILE : (c + 1) * TILE]
            parts.append(
                jnp.where(high, tail[128 * c : 128 * (c + 1)].reshape(NEGS, 8, TILE), own)
            )
        lower = jnp.concatenate(parts, axis=2)
        block = jnp.concatenate([main[:, 0:8, :], lower], axis=1)
        row_send[pl.ds(base, NEGS)] = block.astype(BF16)

        def post(i, carry):
            n = lax.rem(neg + i, NEGS)
            d = g * NEGS + n

            @pl.when(d != me)
            def _():
                pltpu.make_async_remote_copy(
                    src_ref=row_send.at[d],
                    dst_ref=row_recv.at[me],
                    send_sem=row_ssem.at[d],
                    recv_sem=row_rsem.at[me],
                    device_id=(g, n),
                    device_id_type=MESH,
                ).start()

            return carry

        lax.fori_loop(0, NEGS, post, 0)
        return carry

    lax.fori_loop(0, REPS, serve, 0)
    row_recv[me] = row_send[me]

    x = x_v[...]
    for j in range(TILES):
        cw_loads[j].wait()
        mixed_v[:, j * TILE : (j + 1) * TILE] = nn(x, cw_v[j])
    mixed_in = mixed_v[...]
    mixed = jnp.maximum(mixed_in, 0.0)
    inv_mid = lax.rsqrt(jnp.mean(mixed * mixed, axis=1, keepdims=True) + EPSILON)
    normed = mixed * inv_mid
    top_rows = bf(iota((8, B), 0) == iota((8, B), 1))
    hops = nn(top_rows, hop_ref[...].astype(F32).astype(BF16))
    lanes_of = bf(iota((K1, HOP1), 0) == iota((K1, HOP1), 1) % K1)
    own_hop = iota((8, HOP1), 0) == iota((8, HOP1), 1) // K1
    hop_total = jnp.maximum(jnp.sum(hops, axis=1, keepdims=True), 1.0)
    hop_mat = jnp.where(own_hop, nn(hops.astype(BF16), lanes_of), 0.0) / hop_total
    top_in = nn(hop_mat, normed, HIGH)
    inv_top = lax.rsqrt(jnp.mean(top_in * top_in, axis=1, keepdims=True) + EPSILON)
    embedding = (top_in * inv_top).astype(BF16)
    part = H // 4
    packed = jnp.zeros((16, part), F32)
    for c in range(4):
        move = bf(
            (iota((16, 8), 0) == iota((16, 8), 1) + 4 * c) & (iota((16, 8), 1) < B)
        )
        packed = packed + nn(move, embedding[:, c * part : (c + 1) * part])
    emb_send[...] = packed.astype(BF16)

    def peers(body):
        def step(i, carry):
            body(lax.rem(neg + i, NEGS))
            return carry

        lax.fori_loop(1, NEGS, step, 0)

    def copy_to(src, dst, ssem, rsem, where):
        return pltpu.make_async_remote_copy(
            src_ref=src, dst_ref=dst, send_sem=ssem, recv_sem=rsem,
            device_id=where, device_id_type=MESH,
        )

    peers(
        lambda n: copy_to(
            emb_send, emb_all.at[neg], emb_ssem.at[n], emb_rsem.at[neg], (rep, n)
        ).start()
    )
    emb_all[neg] = emb_send[...]
    for b in range(8):
        curt_v[b % 2, 128 * (b // 2) : 128 * (b // 2) + 128, :] = (
            cur_v[:, 128 * b : 128 * b + 128].astype(F32).T.astype(BF16)
        )
    loads[2].wait()
    loads[3].wait()
    peers(
        lambda n: copy_to(
            emb_send, emb_all.at[n], emb_ssem.at[n], emb_rsem.at[n], (rep, neg)
        ).wait()
    )

    gathered = emb_all[...].reshape(256, part)
    row_q, col_q = iota((64, 256), 0), iota((64, 256), 1)
    for c in range(4):
        move = bf(col_q == (row_q // 4) * 16 + 4 * c + row_q % 4)
        e_v[:, c * part : (c + 1) * part] = nn(move, gathered).astype(BF16)
    left = iota((32, 128), 1) < OWN
    scores = jnp.where(left, nt(e_v[0:32, :], cand_v[...]), nt(e_v[32:64, :], cand_v[...]))
    sc_send[...] = scores
    peers(
        lambda n: copy_to(
            sc_send, sc_all.at[neg], sc_ssem.at[n], sc_rsem.at[neg], (rep, n)
        ).start()
    )
    sc_all[neg] = scores
    mates = ids_v[pl.ds(pl.multiple_of(rep * NEGS, NEGS), NEGS), :].astype(BF16)
    halves = []
    for h in range(2):
        pick = bf(iota((32, NEGS), 0) // B + 8 * h == iota((32, NEGS), 1))
        wide = nn(pick, mates)
        at, t = iota((32, 128), 1), iota((32, 128), 0) % B
        halves.append(
            jnp.sum(
                jnp.where(at == 32 + t, wide * 32.0, 0.0) + jnp.where(at == 36 + t, wide, 0.0),
                axis=1,
                keepdims=True,
            )
        )
    positive = jnp.where(left, halves[0], halves[1])
    peers(
        lambda n: copy_to(
            sc_send, sc_all.at[n], sc_ssem.at[n], sc_rsem.at[n], (rep, neg)
        ).wait()
    )

    def by_half(values):
        first = jnp.sum(jnp.where(left, values, 0.0), axis=1, keepdims=True)
        second = jnp.sum(jnp.where(left, 0.0, values), axis=1, keepdims=True)
        return jnp.where(left, first, second)

    all_scores = sc_all[...]
    shape = (NEGS, 32, 128)
    cand_id = (iota(shape, 0) * OWN + iota(shape, 2) % OWN).astype(F32)
    is_pos = cand_id == positive[None]
    pos_score = by_half(jnp.sum(jnp.where(is_pos, all_scores, 0.0), axis=0))
    gaps = all_scores - pos_score[None] + MARGIN
    small = jnp.exp(-jnp.abs(gaps))
    losses = jnp.maximum(gaps, 0.0) + jnp.log1p(small)
    sigmoid = jnp.where(gaps >= 0.0, 1.0, small) / (1.0 + small)
    loss = by_half(jnp.sum(losses, axis=0)) / (NEGS * OWN)
    totals = by_half(jnp.sum(sigmoid, axis=0))
    own_gap = sc_all[neg] - pos_score + MARGIN
    own_small = jnp.exp(-jnp.abs(own_gap))
    own_sig = jnp.where(own_gap >= 0.0, 1.0, own_small) / (1.0 + own_small)
    own_id = (neg * OWN + iota((32, 128), 1) % OWN).astype(F32)
    score_grad = (own_sig - jnp.where(own_id == positive, totals, 0.0)) / (NEGS * OWN)
    lines = (iota((8, 32), 1) == iota((8, 32), 0) + B * (neg % 8)).astype(F32)
    half = jnp.where(neg // 8 == 0, 0, OWN)
    mine = nn(lines, loss, HIGH)
    loss_ref[...] = jnp.sum(
        jnp.where(iota((8, 128), 1) == half, mine, 0.0), axis=1, keepdims=True
    ) + jnp.zeros((8, 128), F32)

    g_left = jnp.where(left, score_grad, 0.0).astype(BF16)
    g_right = jnp.where(left, 0.0, score_grad).astype(BF16)
    eg = jnp.concatenate([nn(g_left, cand_v[...]), nn(g_right, cand_v[...])], axis=0).astype(BF16)
    row_p, col_p = iota((256, 64), 0), iota((256, 64), 1)
    eg_out = jnp.zeros((256, part), F32)
    for c in range(4):
        move = bf((row_p // 16 == col_p // 4) & (row_p % 16 == 4 * c + col_p % 4))
        eg_out = eg_out + nn(move, eg[:, c * part : (c + 1) * part])
    eg_send[...] = eg_out.astype(BF16).reshape(NEGS, 16, part)
    peers(
        lambda n: copy_to(
            eg_send.at[n], eg_recv.at[neg], eg_ssem.at[n], eg_rsem.at[neg], (rep, n)
        ).start()
    )
    eg_recv[neg] = eg_send[neg]
    cand_out[...] = tn(g_left, e_v[0:32, :])[0:OWN] + tn(g_right, e_v[32:64, :])[OWN:128]
    peers(
        lambda n: copy_to(
            eg_send.at[n], eg_recv.at[n], eg_ssem.at[n], eg_rsem.at[n], (rep, neg)
        ).wait()
    )
    eg_sum = jnp.sum(eg_recv[...].astype(F32), axis=0)
    embed_grad = []
    for c in range(4):
        move = (
            (iota((8, 16), 1) == iota((8, 16), 0) + 4 * c) & (iota((8, 16), 0) < B)
        ).astype(F32)
        embed_grad.append(nn(move, eg_sum, HIGH))
    embed_grad = jnp.concatenate(embed_grad, axis=1)

    top_grad = inv_top * embed_grad - top_in * (
        inv_top * inv_top * inv_top * jnp.mean(embed_grad * top_in, axis=1, keepdims=True)
    )
    normed_grad = tn(hop_mat, top_grad, HIGH)
    mixed_grad = inv_mid * normed_grad - mixed * (
        inv_mid * inv_mid * inv_mid * jnp.mean(normed_grad * mixed, axis=1, keepdims=True)
    )
    mixed_in_grad = jnp.where(mixed_in > 0.0, mixed_grad, 0.0).astype(BF16)
    total = jnp.zeros((HOP1, H), F32)
    for j in range(TILES):
        total = total + nt(mixed_in_grad[:, j * TILE : (j + 1) * TILE], cw_v[j, F : F + H, :])
    pooled_g[...] = total

    other = (y * CORES + 1 - core, neg)
    for j in range(TILES):
        spread_grad = jnp.broadcast_to(
            pooled_g[:, j * TILE : (j + 1) * TILE][:, None, :], (HOP1, SLOTS, TILE)
        ).reshape(REQ, TILE)
        pgrad_v[...] = jnp.where(mask_v[j].astype(F32) > 0.0, spread_grad * weight, 0.0).astype(
            BF16
        )
        p_send[j] = nn(curt_v[1 - core], pgrad_v[...]).astype(BF16)
        copy_to(p_send.at[j], p_recv.at[j], p_ssem.at[j], p_rsem.at[j], other).start()
        p_own[j] = nn(curt_v[core], pgrad_v[...])

    half_tiles = TILES // 2

    def y_peers(body):
        def step(i, carry):
            body(lax.rem(y + i, YS))
            return carry

        lax.fori_loop(1, YS, step, 0)

    for j in range(TILES):
        copy_to(p_send.at[j], p_recv.at[j], p_ssem.at[j], p_rsem.at[j], other).wait()
        chip_sum = p_own[j] + p_recv[j].astype(F32)
        if j < half_tiles:
            a1_send[j] = chip_sum.astype(BF16).reshape(YS, 128, TILE)
            y_peers(
                lambda q, j=j: copy_to(
                    a1_send.at[j, q], a1_recv.at[j, y], a1_ssem.at[j, q], a1_rsem.at[j, y],
                    (q * CORES + core, neg),
                ).start()
            )
            a1_recv[j, y] = a1_send[j, y]
        else:
            k = j - half_tiles
            for q in range(YS):
                b1_f[:, 8 * q : 8 * q + 8, :] = chip_sum[128 * q : 128 * q + 128].reshape(
                    NEGS, 8, TILE
                )
            b1_send[k] = b1_f[...].astype(BF16)
            peers(
                lambda n, k=k: copy_to(
                    b1_send.at[k, n], b1_recv.at[k, neg], b1_ssem.at[k, n], b1_rsem.at[k, neg],
                    (rep, n),
                ).start()
            )
            b1_recv[k, neg] = b1_send[k, neg]

    for j in range(half_tiles):
        y_peers(
            lambda q, j=j: copy_to(
                a1_send.at[j, q], a1_recv.at[j, q], a1_ssem.at[j, q], a1_rsem.at[j, q],
                (rep, neg),
            ).wait()
        )
        a2_f[:, 8 * j : 8 * j + 8, :] = jnp.sum(a1_recv[j].astype(F32), axis=0).reshape(
            NEGS, 8, TILE
        )
    a2_send[...] = a2_f[...].astype(BF16)
    peers(
        lambda n: copy_to(
            a2_send.at[n], a2_recv.at[neg], a2_ssem.at[n], a2_rsem.at[neg], (rep, n)
        ).start()
    )
    a2_recv[neg] = a2_send[neg]
    for k in range(half_tiles):
        peers(
            lambda n, k=k: copy_to(
                b1_send.at[k, n], b1_recv.at[k, n], b1_ssem.at[k, n], b1_rsem.at[k, n],
                (rep, neg),
            ).wait()
        )
        b2_f[:, 8 * k : 8 * k + 8, :] = jnp.sum(b1_recv[k].astype(F32), axis=0).reshape(
            YS, 8, TILE
        )
    b2_send[...] = b2_f[...].astype(BF16)
    y_peers(
        lambda q: copy_to(
            b2_send.at[q], b2_recv.at[y], b2_ssem.at[q], b2_rsem.at[y], (q * CORES + core, neg)
        ).start()
    )
    b2_recv[y] = b2_send[y]

    owner_col = cols_v[:, 0:1]
    rank_col = cols_v[:, 1:2]
    third = jnp.floor((rank_col + 0.5) * (1.0 / 3.0))
    left_over = rank_col - 3.0 * third
    slot_main = owner_col * 16.0 + rank_col
    slot_tail = owner_col * 16.0 + 12.0 + third

    def place(step, carry):
        g = lax.rem(rep - step + REPS, REPS)

        def arrive(i, carry):
            d = g * NEGS + lax.rem(neg + i, NEGS)

            @pl.when(d != me)
            def _():
                copy_to(
                    row_send.at[d], row_recv.at[d], row_ssem.at[d], row_rsem.at[d], (rep, neg)
                ).wait()

            return carry

        lax.fori_loop(0, NEGS, arrive, 0)
        block = row_recv[pl.ds(pl.multiple_of(g * NEGS, NEGS), NEGS)].reshape(256, WIDE)
        line = (iota((REQ, 256), 1) + g * 256).astype(F32)
        new = [nn(bf(line == slot_main), block)]
        tail = jnp.zeros((REQ, TILE), F32)
        for c in range(3):
            pick = bf((line == slot_tail) & (left_over == float(c)))
            tail = tail + nn(pick, block[:, c * TILE : (c + 1) * TILE])
        new = jnp.concatenate(new + [tail], axis=1).astype(BF16)

        @pl.when(step == 0)
        def _():
            rows_acc[...] = new

        @pl.when(step > 0)
        def _():
            rows_acc[...] = rows_acc[...] + new

        return carry

    lax.fori_loop(0, REPS, place, 0)
    out = pltpu.make_async_copy(rows_acc, rows_hbm, out_sem)
    out.start()

    peers(
        lambda n: copy_to(
            a2_send.at[n], a2_recv.at[n], a2_ssem.at[n], a2_rsem.at[n], (rep, neg)
        ).wait()
    )
    y_peers(
        lambda q: copy_to(
            b2_send.at[q], b2_recv.at[q], b2_ssem.at[q], b2_rsem.at[q], (rep, neg)
        ).wait()
    )
    a_sum = jnp.sum(a2_recv[...].astype(F32), axis=0)
    b_sum = jnp.sum(b2_recv[...].astype(F32), axis=0)
    for j in range(half_tiles):
        ngrad_ref[:, j * TILE : (j + 1) * TILE] = a_sum[8 * j : 8 * j + 8]
        ngrad_ref[:, (j + half_tiles) * TILE : (j + half_tiles + 1) * TILE] = b_sum[
            8 * j : 8 * j + 8
        ]
    out.wait()


def local(
    feature_table, cur_rows, next_owner, next_local, slot_counts, hop_counts, positive_ids,
    neighbor_weight, combine_weight, candidates,
):
    vmem = pl.BlockSpec(memory_space=pltpu.VMEM)
    smem = pl.BlockSpec(memory_space=pltpu.SMEM)
    hbm = pl.BlockSpec(memory_space=pl.ANY)
    dma = pltpu.SemaphoreType.DMA
    part = H // 4
    scratch = [
        pltpu.VMEM((REQ, F), BF16),
        pltpu.VMEM((2, 512, REQ), BF16),
        pltpu.VMEM((F, F), BF16),
        pltpu.VMEM((TILES, F, TILE), BF16),
        pltpu.VMEM((TILES, F + H, TILE), BF16),
        pltpu.VMEM((2 * OWN, H), BF16),
        pltpu.VMEM((TILES, REQ, TILE), BF16),
        pltpu.VMEM((REQ, TILE), BF16),
        pltpu.VMEM((HOP1, F + H), BF16),
        pltpu.VMEM((HOP1, H), F32),
        pltpu.VMEM((HOP1, H), F32),
        pltpu.VMEM((DEVS, 1, 128), F32),
        pltpu.VMEM((DEVS, 1, 128), F32),
        pltpu.VMEM((DEVS, 128), F32),
        pltpu.VMEM((DEVS, 16, WIDE), BF16),
        pltpu.VMEM((DEVS, 16, WIDE), BF16),
        pltpu.VMEM((REQ, F), BF16),
        pltpu.VMEM((REQ, 16), F32),
        pltpu.VMEM((16, part), BF16),
        pltpu.VMEM((NEGS, 16, part), BF16),
        pltpu.VMEM((64, H), BF16),
        pltpu.VMEM((32, 128), F32),
        pltpu.VMEM((NEGS, 32, 128), F32),
        pltpu.VMEM((NEGS, 16, part), BF16),
        pltpu.VMEM((NEGS, 16, part), BF16),
        pltpu.VMEM((TILES, 512, TILE), BF16),
        pltpu.VMEM((TILES, 512, TILE), BF16),
        pltpu.VMEM((TILES, 512, TILE), F32),
        pltpu.VMEM((4, YS, 128, TILE), BF16),
        pltpu.VMEM((4, YS, 128, TILE), BF16),
        pltpu.VMEM((NEGS, 32, TILE), F32),
        pltpu.VMEM((NEGS, 32, TILE), BF16),
        pltpu.VMEM((NEGS, 32, TILE), BF16),
        pltpu.VMEM((NEGS, 32, TILE), F32),
        pltpu.VMEM((4, NEGS, 32, TILE), BF16),
        pltpu.VMEM((4, NEGS, 32, TILE), BF16),
        pltpu.VMEM((YS, 32, TILE), F32),
        pltpu.VMEM((YS, 32, TILE), BF16),
        pltpu.VMEM((YS, 32, TILE), BF16),
        dma((20,)), dma(()),
        dma((DEVS,)), dma((DEVS,)), dma((DEVS,)), dma((DEVS,)),
        dma((NEGS,)), dma((NEGS,)), dma((NEGS,)), dma((NEGS,)), dma((NEGS,)), dma((NEGS,)),
        dma((TILES,)), dma((TILES,)),
        dma((4, YS)), dma((4, YS)),
        dma((NEGS,)), dma((NEGS,)),
        dma((4, NEGS)), dma((4, NEGS)),
        dma((YS,)), dma((YS,)),
    ]
    next_rows, loss, cand_grad, neighbor_grad = pl.pallas_call(
        kernel,
        out_shape=(
            jax.ShapeDtypeStruct((REQ, F), BF16),
            jax.ShapeDtypeStruct((8, 128), F32),
            jax.ShapeDtypeStruct((OWN, H), F32),
            jax.ShapeDtypeStruct((8, H), F32),
        ),
        in_specs=[vmem, vmem, vmem, vmem, smem, hbm, hbm, hbm, hbm, hbm],
        out_specs=(hbm, vmem, vmem, vmem),
        scratch_shapes=scratch,
        compiler_params=pltpu.CompilerParams(
            collective_id=0, has_side_effects=True, vmem_limit_bytes=62 * 2**20
        ),
        name="step",
    )(
        next_owner.reshape(1, REQ),
        next_local.reshape(1, REQ),
        slot_counts.T,
        hop_counts,
        positive_ids.reshape(1, B),
        feature_table,
        cur_rows,
        neighbor_weight,
        combine_weight,
        candidates,
    )
    return next_rows, loss[:B, 0], cand_grad, neighbor_grad


def solution(mesh):
    both = P(("rep", "neg"), None)
    flat = P(("rep", "neg"))
    return jax.shard_map(
        local,
        mesh=mesh,
        in_specs=(both, both, both, flat, both, both, flat, P(), P(), both),
        out_specs=(both, flat, both, both),
        check_vma=False,
    )
```

time: 878 us -> 143 us (0.16)
  waiting for transfers between devices: 661 us -> 0 us
  Pallas kernels: 0 us -> 135 us
  blocking collectives: 76 us -> 0 us
  local copies, waits for them, and re-layouts: 76.2 us -> 6.75 us
  matrix products: 40 us -> 0 us
  between operations: 14 us -> 0.65 us
  other arithmetic: 11.7 us -> 0 us
    unnamed x4 -> x0, waiting for transfers between devices: 543 us -> none
    pallas_call x0 -> x1, Pallas kernels: none -> 135 us  [local(): pl.pallas_call(kernel, out_shape=(jax.ShapeDtypeStruct((REQ, F), BF16), j...]
    reduce_scatter x1 -> x0, waiting for transfers between devices: 83.6 us -> none  [local(): lax.psum_scatter(lax.dot_general(score_grad, embedding, (((0,), (0,)), ((...]
    all_to_all x2 -> x0, blocking collectives: 76 us -> none  [the longest x1 58.4 us: local(): lax.all_to_all(jnp.where(present[..., None], fetched, jnp.zeros_like(fetc...]
    dot_general x8 -> x0, matrix products: 40 us -> none  [the longest x1 8.76 us: local(): jnp.dot(cur_rows, neighbor_weight, preferred_element_type=jnp.float32)]
    scatter x1 -> x0, local copies, waits for them, and re-layouts: 36.6 us -> none  [local(): jnp.full((devices, capacity), -1, jnp.int32).at[owner_ids, slot_rank]]
    all_gather x1 -> x0, waiting for transfers between devices: 33.8 us -> none  [local(): cand_all = lax.all_gather(candidates, 'neg', axis=0, tiled=True)]
    gather x4 -> x0, local copies, waits for them, and re-layouts: 24 us -> none  [the longest x2 11.9 us: local(): fetched = feature_table[jnp.maximum(asked, 0)]]
  transfers between devices with their start and end apart: 3 -> 0, of which waited for: 3 -> 0; matrix products, arithmetic and copies ran while one was open for 11% -> 0% of each run, Pallas kernels for 0% -> 0%
where the time goes in v2:
time: 143 us; the launch traced here: 142 us
  Pallas kernels  135 us (94%)
  local copies, waits for them, and re-layouts  6.75 us (5%)
    pallas_call x1, Pallas kernels, local(): pl.pallas_call(kernel, out_shape=(jax.ShapeDtypeStruct((REQ, F), BF16), j...  135 us
    unnamed x7, local copies, waits for them, and re-layouts  4.13 us

profile of v2, /device:TPU:0, one launch (start us, length us, event | category | flops | bytes accessed | tf_op | source)
XLA Modules:
  0.0 142.4 jit_solution(17140004137082726685)
XLA Ops:
  0.6 1.3 reshape.18.local_ref
  1.9 135.0 %step.1 = (bf16[768,1024]{1,0:T(8,128)(2,1)}, f32[8,128]{1,0:T(8,128)}, f32[64,2048]{1,0:T(8,128)}, f32[8,2048]{1,0:T(8,128)}) custom-call(s32[1,768]{1,0:T(1,128)} %bitcast.4, s32[1,768]{1,0:T(1,128)} %reshape.18.local_ref, s32[16,48]{1,0:T(8,128)} %bitcast.3, s32[4,12]{1,0:T(4,128)} %hop_ref.1, s32[1,4]{1,0:T(1,128)} %bitcast.5, ...), custom_call_target="tpu_custom_call" | custom-call | tf_op jit(solution)/shard_map/step/pallas_call | solution.py:601
  136.9 0.0 copy-start
  136.9 1.4 slice_reduce_fusion
  138.3 0.0 copy-start.1
  138.3 2.7 %copy.17 = bf16[768,1024]{1,0:T(8,128)(2,1)} copy(bf16[768,1024]{1,0:T(8,128)(2,1)} %get-tuple-element.16) | data formatting | bytes 3145728
  141.0 0.0 copy-done
  141.0 0.8 copy.18
  141.8 0.0 copy-done.1
  141.8 0.6 copy.19
Async XLA Ops:
  136.9 4.1 %copy-start = (f32[64,2048]{1,0:T(8,128)S(1)}, f32[64,2048]{1,0:T(8,128)}, u32[]{:S(2)}) copy-start(f32[64,2048]{1,0:T(8,128)} %get-tuple-element.18) | copy-start | bytes 1572868
  138.3 3.5 %copy-start.1 = (f32[8,2048]{1,0:T(8,128)S(1)}, f32[8,2048]{1,0:T(8,128)}, u32[]{:S(2)}) copy-start(f32[8,2048]{1,0:T(8,128)} %get-tuple-element.19) | copy-start | bytes 196612

commit v3 on v2

v3 whole, which is shorter than its diff:
```python
import jax
import jax.numpy as jnp
from jax import lax
from jax.experimental import pallas as pl
from jax.experimental.pallas import tpu as pltpu
from jax.sharding import PartitionSpec as P

EPSILON = 1e-06
MARGIN = 0.5
MESH = pl.DeviceIdType.MESH
F32 = jnp.float32
BF16 = jnp.bfloat16
HIGH = lax.Precision.HIGHEST

REPS, NEGS, DEVS = 8, 16, 128
YS, CORES = 4, 2
F, H = 1024, 2048
TILE = 512
TILES = H // TILE
REQ, HOP1, SLOTS, B, K1 = 768, 48, 16, 4, 12
PART = 256
WIDE = 3 * PART
OWN = 64


def iota(shape, dim):
    return lax.broadcasted_iota(jnp.int32, shape, dim)


def nt(a, b, precision=None):
    return lax.dot_general(
        a, b, (((1,), (1,)), ((), ())), preferred_element_type=F32, precision=precision
    )


def tn(a, b, precision=None):
    return lax.dot_general(
        a, b, (((0,), (0,)), ((), ())), preferred_element_type=F32, precision=precision
    )


def nn(a, b, precision=None):
    return jnp.dot(a, b, preferred_element_type=F32, precision=precision)


def bf(mask):
    return mask.astype(F32).astype(BF16)


def kernel(
    owner_ref, local_ref, slot_ref, hop_ref, pos_ref,
    table_hbm, cur_hbm, nw_hbm, cw_hbm, cand_hbm,
    rows_hbm, loss_ref, cand_out, ngrad_ref,
    cur_v, curt_v, table_v, nw_v, cw_v, cand_v, mask_v, pgrad_v, x_v, mixed_v, pooled_g,
    ask_send, ask_mid, ask_recv, ids_v, row_out, row_send, row_recv, rows_acc, cols_v,
    emb_send, emb_all, e_v, sc_send, sc_all, eg_send, eg_recv,
    p_send, p_recv, p_own, a1_send, a1_recv, a2_f, a2_send, a2_recv,
    b1_f, b1_send, b1_recv, b2_f, b2_send, b2_recv,
    in_sem, out_sem, ask_sem, out_ssem, out_rsem, row_ssem, row_rsem,
    emb_sem, sc_sem, eg_sem, p_ssem, p_rsem, a1_ssem, a1_rsem, a2_sem, b1_ssem, b1_rsem, b2_sem,
):
    rep = lax.axis_index("rep")
    neg = lax.axis_index("neg")
    y, core = rep // CORES, rep % CORES
    mate = (y * CORES + 1 - core, neg)

    def send(src, dst, ssem, rsem, where):
        pltpu.make_async_remote_copy(
            src_ref=src, dst_ref=dst, send_sem=ssem, recv_sem=rsem,
            device_id=where, device_id_type=MESH,
        ).start()

    def settle(ref, sem):
        pltpu.make_async_copy(ref, ref, sem).wait()

    def around(here, count, body):
        def step(i, carry):
            body(lax.rem(here + i, count))
            return carry

        lax.fori_loop(1, count, step, 0)

    loads = [
        pltpu.make_async_copy(cur_hbm, cur_v, in_sem.at[0]),
        pltpu.make_async_copy(table_hbm, table_v, in_sem.at[1]),
        pltpu.make_async_copy(cand_hbm, cand_v.at[pl.ds(0, OWN)], in_sem.at[2]),
        pltpu.make_async_copy(cand_hbm, cand_v.at[pl.ds(OWN, OWN)], in_sem.at[3]),
    ]
    nw_loads = [
        pltpu.make_async_copy(
            nw_hbm.at[:, pl.ds(j * TILE, TILE)], nw_v.at[j], in_sem.at[4 + j]
        )
        for j in range(TILES)
    ]
    cw_loads = [
        pltpu.make_async_copy(
            cw_hbm.at[:, pl.ds(j * TILE, TILE)], cw_v.at[j], in_sem.at[4 + TILES + j]
        )
        for j in range(TILES)
    ]
    loads[0].start()
    for load in nw_loads:
        load.start()
    for load in loads[1:]:
        load.start()
    for load in cw_loads:
        load.start()

    barrier = pltpu.get_barrier_semaphore()

    def greet(where):
        pl.semaphore_signal(barrier, inc=1, device_id=where, device_id_type=MESH)

    around(neg, NEGS, lambda n: greet((rep, n)))
    around(rep, REPS, lambda r: greet((r, neg)))

    owner = owner_ref[...]
    hit = owner == iota((DEVS, REQ), 0)
    hit_low = bf(hit)
    before = bf(iota((REQ, REQ), 0) < iota((REQ, REQ), 1))
    count = nn(hit_low, before)
    rank = jnp.sum(jnp.where(hit, count, 0.0), axis=0, keepdims=True)
    local = local_ref[...].reshape(1, REQ)
    line = iota((DEVS, REQ), 0).astype(F32)
    pay = jnp.where(line == rank, (local >> 5).astype(F32), 0.0) + jnp.where(
        line == rank + 16.0, (local & 31).astype(F32), 0.0
    )
    asks = nt(hit_low, pay.astype(BF16))
    lane1 = iota((1, 128), 1)
    positives = jnp.zeros((1, 128), jnp.int32)
    for t in range(B):
        value = pos_ref[t]
        positives = positives + jnp.where(lane1 == 32 + t, value >> 5, 0)
        positives = positives + jnp.where(lane1 == 36 + t, value & 31, 0)
    asks = asks + positives.astype(F32)
    ask_send[...] = asks.reshape(REPS, NEGS, 1, 128)

    pl.semaphore_wait(barrier, NEGS - 1 + REPS - 1)
    around(
        rep, REPS,
        lambda r: send(
            ask_send.at[r], ask_mid.at[rep], ask_sem.at[0], ask_sem.at[1], (r, neg)
        ),
    )
    ask_mid[rep] = ask_send[rep]

    placed = (owner >> 5) * 32 + (owner & 15) * 2 + ((owner >> 4) & 1)
    eye = bf(iota((REQ, REQ), 0) == iota((REQ, REQ), 1))
    pair = jnp.where(iota((16, REQ), 0) == 0, placed.astype(F32), rank).astype(BF16)
    cols_v[...] = nt(eye, pair)

    spread = bf(iota((REQ, HOP1), 0) // SLOTS == iota((REQ, HOP1), 1))
    counts = nt(spread, slot_ref[...].astype(F32).astype(BF16))
    at_slot = iota((REQ, SLOTS), 0) % SLOTS == iota((REQ, SLOTS), 1)
    weight = jnp.sum(jnp.where(at_slot, counts, 0.0), axis=1, keepdims=True) / jnp.sum(
        counts, axis=1, keepdims=True
    )

    loads[0].wait()

    def project(j):
        nw_loads[j].wait()
        projected = nn(cur_v[...], nw_v[j])
        mask_v[j] = bf(projected > 0.0)
        weighted = jnp.maximum(projected, 0.0) * weight
        pooled = jnp.sum(weighted.reshape(HOP1, SLOTS, TILE), axis=1)
        x_v[:, F + j * TILE : F + (j + 1) * TILE] = pooled.astype(BF16)

    for j in range(TILES // 2):
        project(j)
    settle(ask_mid.at[pl.ds(0, REPS - 1)], ask_sem.at[1])
    around(
        neg, NEGS,
        lambda n: send(
            ask_mid.at[:, n], ask_recv.at[:, neg], ask_sem.at[2], ask_sem.at[3], (rep, n)
        ),
    )
    ask_recv[:, neg] = ask_mid[:, neg]
    for j in range(TILES // 2, TILES):
        project(j)
    first = bf(iota((HOP1, REQ), 0) * SLOTS == iota((HOP1, REQ), 1))
    x_v[:, 0:F] = nn(first, cur_v[...]).astype(BF16)
    loads[1].wait()
    settle(ask_recv.at[:, pl.ds(0, NEGS - 1)], ask_sem.at[3])
    ids_v[...] = ask_recv[...].reshape(DEVS, 128)

    def serve(g):
        base = pl.multiple_of(g * NEGS, NEGS)
        asked = ids_v[pl.ds(base, NEGS), :].astype(BF16)

        def chosen(rows, per, slot_of):
            wide = nn(bf(iota((rows, NEGS), 0) // per % NEGS == iota((rows, NEGS), 1)), asked)
            slot = slot_of(iota((rows, 1), 0))
            at = iota((rows, 128), 1)
            ids = jnp.sum(
                jnp.where(at == slot, wide * 32.0, 0.0) + jnp.where(at == slot + 16, wide, 0.0),
                axis=1,
                keepdims=True,
            )
            return bf(ids == iota((rows, F), 1).astype(F32))

        main = nn(chosen(256, 16, lambda r: r % 16), table_v[:, 0:WIDE]).reshape(NEGS, 16, WIDE)
        tail = nn(
            chosen(384, 8, lambda r: jnp.maximum(r % 8 - 4, 0) * 3 + r // 128),
            table_v[:, WIDE:F],
        )
        high = iota((NEGS, 8, PART), 1) >= 4
        parts = []
        for c in range(3):
            own = main[:, 8:16, c * PART : (c + 1) * PART]
            parts.append(
                jnp.where(high, tail[128 * c : 128 * (c + 1)].reshape(NEGS, 8, PART), own)
            )
        lower = jnp.concatenate(parts, axis=2)
        return jnp.concatenate([main[:, 0:8, :], lower], axis=1).astype(BF16)

    def round_of(k):
        to_y = lax.rem(y + k, YS)
        row_out[k] = serve(to_y * CORES + 1 - core)
        send(row_out.at[k], row_send.at[to_y, :, core], out_ssem.at[k], out_rsem.at[k], mate)
        row_send[to_y, :, core] = serve(to_y * CORES + core)
        settle(row_out.at[k], out_rsem.at[k])

        def post(n):
            send(
                row_send.at[to_y, n], row_recv.at[y, neg], row_ssem.at[k], row_rsem.at[y],
                (to_y * CORES + core, n),
            )

        around(neg, NEGS, post)
        if k == 0:
            row_recv[y, neg] = row_send[y, neg]
        else:
            post(neg)

    round_of(0)

    x = x_v[...]
    for j in range(TILES):
        cw_loads[j].wait()
        mixed_v[:, j * TILE : (j + 1) * TILE] = nn(x, cw_v[j])
    mixed_in = mixed_v[...]
    mixed = jnp.maximum(mixed_in, 0.0)
    inv_mid = lax.rsqrt(jnp.mean(mixed * mixed, axis=1, keepdims=True) + EPSILON)
    normed = mixed * inv_mid
    top_rows = bf(iota((8, B), 0) == iota((8, B), 1))
    hops = nn(top_rows, hop_ref[...].astype(F32).astype(BF16))
    lanes_of = bf(iota((K1, HOP1), 0) == iota((K1, HOP1), 1) % K1)
    own_hop = iota((8, HOP1), 0) == iota((8, HOP1), 1) // K1
    hop_total = jnp.maximum(jnp.sum(hops, axis=1, keepdims=True), 1.0)
    hop_mat = jnp.where(own_hop, nn(hops.astype(BF16), lanes_of), 0.0) / hop_total
    top_in = nn(hop_mat, normed, HIGH)
    inv_top = lax.rsqrt(jnp.mean(top_in * top_in, axis=1, keepdims=True) + EPSILON)
    embedding = (top_in * inv_top).astype(BF16)
    part = H // 4
    packed = jnp.zeros((16, part), F32)
    for c in range(4):
        move = bf(
            (iota((16, 8), 0) == iota((16, 8), 1) + 4 * c) & (iota((16, 8), 1) < B)
        )
        packed = packed + nn(move, embedding[:, c * part : (c + 1) * part])
    emb_send[...] = packed.astype(BF16)
    around(
        neg, NEGS,
        lambda n: send(emb_send, emb_all.at[neg], emb_sem.at[0], emb_sem.at[1], (rep, n)),
    )
    emb_all[neg] = emb_send[...]

    round_of(1)

    loads[2].wait()
    loads[3].wait()
    settle(emb_all.at[pl.ds(0, NEGS - 1)], emb_sem.at[1])

    gathered = emb_all[...].reshape(256, part)
    row_q, col_q = iota((64, 256), 0), iota((64, 256), 1)
    for c in range(4):
        move = bf(col_q == (row_q // 4) * 16 + 4 * c + row_q % 4)
        e_v[:, c * part : (c + 1) * part] = nn(move, gathered).astype(BF16)
    left = iota((32, 128), 1) < OWN
    scores = jnp.where(left, nt(e_v[0:32, :], cand_v[...]), nt(e_v[32:64, :], cand_v[...]))
    sc_send[...] = scores
    around(
        neg, NEGS,
        lambda n: send(sc_send, sc_all.at[neg], sc_sem.at[0], sc_sem.at[1], (rep, n)),
    )
    sc_all[neg] = scores

    round_of(2)

    mates = ids_v[pl.ds(pl.multiple_of(rep * NEGS, NEGS), NEGS), :].astype(BF16)
    halves = []
    for h in range(2):
        pick = bf(iota((32, NEGS), 0) // B + 8 * h == iota((32, NEGS), 1))
        wide = nn(pick, mates)
        at, t = iota((32, 128), 1), iota((32, 128), 0) % B
        halves.append(
            jnp.sum(
                jnp.where(at == 32 + t, wide * 32.0, 0.0) + jnp.where(at == 36 + t, wide, 0.0),
                axis=1,
                keepdims=True,
            )
        )
    positive = jnp.where(left, halves[0], halves[1])
    settle(sc_all.at[pl.ds(0, NEGS - 1)], sc_sem.at[1])

    def by_half(values):
        first = jnp.sum(jnp.where(left, values, 0.0), axis=1, keepdims=True)
        second = jnp.sum(jnp.where(left, 0.0, values), axis=1, keepdims=True)
        return jnp.where(left, first, second)

    all_scores = sc_all[...]
    shape = (NEGS, 32, 128)
    cand_id = (iota(shape, 0) * OWN + iota(shape, 2) % OWN).astype(F32)
    is_pos = cand_id == positive[None]
    pos_score = by_half(jnp.sum(jnp.where(is_pos, all_scores, 0.0), axis=0))
    gaps = all_scores - pos_score[None] + MARGIN
    small = jnp.exp(-jnp.abs(gaps))
    losses = jnp.maximum(gaps, 0.0) + jnp.log1p(small)
    sigmoid = jnp.where(gaps >= 0.0, 1.0, small) / (1.0 + small)
    loss = by_half(jnp.sum(losses, axis=0)) / (NEGS * OWN)
    totals = by_half(jnp.sum(sigmoid, axis=0))
    own_gap = sc_all[neg] - pos_score + MARGIN
    own_small = jnp.exp(-jnp.abs(own_gap))
    own_sig = jnp.where(own_gap >= 0.0, 1.0, own_small) / (1.0 + own_small)
    own_id = (neg * OWN + iota((32, 128), 1) % OWN).astype(F32)
    score_grad = (own_sig - jnp.where(own_id == positive, totals, 0.0)) / (NEGS * OWN)

    g_left = jnp.where(left, score_grad, 0.0).astype(BF16)
    g_right = jnp.where(left, 0.0, score_grad).astype(BF16)
    eg = jnp.concatenate([nn(g_left, cand_v[...]), nn(g_right, cand_v[...])], axis=0).astype(BF16)
    row_p, col_p = iota((256, 64), 0), iota((256, 64), 1)
    eg_out = jnp.zeros((256, part), F32)
    for c in range(4):
        move = bf((row_p // 16 == col_p // 4) & (row_p % 16 == 4 * c + col_p % 4))
        eg_out = eg_out + nn(move, eg[:, c * part : (c + 1) * part])
    eg_send[...] = eg_out.astype(BF16).reshape(NEGS, 16, part)
    around(
        neg, NEGS,
        lambda n: send(eg_send.at[n], eg_recv.at[neg], eg_sem.at[0], eg_sem.at[1], (rep, n)),
    )
    eg_recv[neg] = eg_send[neg]

    round_of(3)

    lines = (iota((32, 128), 0) == iota((32, 128), 1) + B * (neg % 8)).astype(F32)
    half = jnp.where(neg // 8 == 0, 0, OWN)
    mine = tn(loss, lines, HIGH)
    loss_ref[...] = jnp.sum(
        jnp.where(iota((128, 128), 0) == half, mine, 0.0), axis=0, keepdims=True
    )[:, 0:B]
    cand_out[...] = tn(g_left, e_v[0:32, :])[0:OWN] + tn(g_right, e_v[32:64, :])[OWN:128]
    for b in range(8):
        curt_v[b % 2, 128 * (b // 2) : 128 * (b // 2) + 128, :] = (
            cur_v[:, 128 * b : 128 * b + 128].astype(F32).T.astype(BF16)
        )
    settle(eg_recv.at[pl.ds(0, NEGS - 1)], eg_sem.at[1])
    eg_sum = jnp.sum(eg_recv[...].astype(F32), axis=0)
    embed_grad = []
    for c in range(4):
        move = (
            (iota((8, 16), 1) == iota((8, 16), 0) + 4 * c) & (iota((8, 16), 0) < B)
        ).astype(F32)
        embed_grad.append(nn(move, eg_sum, HIGH))
    embed_grad = jnp.concatenate(embed_grad, axis=1)

    top_grad = inv_top * embed_grad - top_in * (
        inv_top * inv_top * inv_top * jnp.mean(embed_grad * top_in, axis=1, keepdims=True)
    )
    normed_grad = tn(hop_mat, top_grad, HIGH)
    mixed_grad = inv_mid * normed_grad - mixed * (
        inv_mid * inv_mid * inv_mid * jnp.mean(normed_grad * mixed, axis=1, keepdims=True)
    )
    mixed_in_grad = jnp.where(mixed_in > 0.0, mixed_grad, 0.0).astype(BF16)
    total = jnp.zeros((HOP1, H), F32)
    for j in range(TILES):
        total = total + nt(mixed_in_grad[:, j * TILE : (j + 1) * TILE], cw_v[j, F : F + H, :])
    pooled_g[...] = total

    order = (0, 2, 1, 3)
    for j in order:
        spread_grad = jnp.broadcast_to(
            pooled_g[:, j * TILE : (j + 1) * TILE][:, None, :], (HOP1, SLOTS, TILE)
        ).reshape(REQ, TILE)
        pgrad_v[...] = jnp.where(mask_v[j].astype(F32) > 0.0, spread_grad * weight, 0.0).astype(
            BF16
        )
        p_send[j] = nn(curt_v[1 - core], pgrad_v[...]).astype(BF16)
        send(p_send.at[j], p_recv.at[j], p_ssem.at[j], p_rsem.at[j], mate)
        p_own[j] = nn(curt_v[core], pgrad_v[...])

    for j in order:
        settle(p_recv.at[j], p_rsem.at[j])
        chip_sum = p_own[j] + p_recv[j].astype(F32)
        if j < 2:
            a1_send[j] = chip_sum.astype(BF16).reshape(YS, 128, TILE)
            around(
                y, YS,
                lambda q, j=j: send(
                    a1_send.at[j, q], a1_recv.at[j, y], a1_ssem.at[j], a1_rsem.at[j],
                    (q * CORES + core, neg),
                ),
            )
            a1_recv[j, y] = a1_send[j, y]
        else:
            k = j - 2
            for q in range(YS):
                b1_f[:, 8 * q : 8 * q + 8, :] = chip_sum[128 * q : 128 * q + 128].reshape(
                    NEGS, 8, TILE
                )
            b1_send[k] = b1_f[...].astype(BF16)
            around(
                neg, NEGS,
                lambda n, k=k: send(
                    b1_send.at[k, n], b1_recv.at[k, neg], b1_ssem.at[k], b1_rsem.at[k], (rep, n)
                ),
            )
            b1_recv[k, neg] = b1_send[k, neg]

    owner_col = cols_v[:, 0:1]
    rank_col = cols_v[:, 1:2]
    third = jnp.floor((rank_col + 0.5) * (1.0 / 3.0))
    left_over = rank_col - 3.0 * third
    slot_main = owner_col * 16.0 + rank_col
    slot_tail = [
        jnp.where(left_over == float(c), owner_col * 16.0 + 12.0 + third, -1.0) for c in range(3)
    ]

    def place(k):
        from_y = lax.rem(y - k + YS, YS)
        got = NEGS - 1 if k == 0 else NEGS
        settle(row_recv.at[from_y, pl.ds(0, got)], row_rsem.at[from_y])
        block = row_recv[from_y].reshape(512, WIDE)
        line = (iota((REQ, 512), 1) + from_y * 512).astype(F32)
        body = nn(bf(line == slot_main), block)
        tail = jnp.zeros((REQ, PART), F32)
        for c in range(3):
            tail = tail + nn(bf(line == slot_tail[c]), block[:, c * PART : (c + 1) * PART])
        new = jnp.concatenate([body, tail], axis=1).astype(BF16)
        rows_acc[...] = new if k == 0 else rows_acc[...] + new

    place(0)
    place(1)

    for j in range(2):
        settle(a1_recv.at[j, pl.ds(0, YS - 1)], a1_rsem.at[j])
        a2_f[:, 8 * j : 8 * j + 8, :] = jnp.sum(a1_recv[j].astype(F32), axis=0).reshape(
            NEGS, 8, TILE
        )
    a2_send[...] = a2_f[...].astype(BF16)
    around(
        neg, NEGS,
        lambda n: send(a2_send.at[n], a2_recv.at[neg], a2_sem.at[0], a2_sem.at[1], (rep, n)),
    )
    a2_recv[neg] = a2_send[neg]
    for k in range(2):
        settle(b1_recv.at[k, pl.ds(0, NEGS - 1)], b1_rsem.at[k])
        b2_f[:, 8 * k : 8 * k + 8, :] = jnp.sum(b1_recv[k].astype(F32), axis=0).reshape(
            YS, 8, TILE
        )
    b2_send[...] = b2_f[...].astype(BF16)
    around(
        y, YS,
        lambda q: send(
            b2_send.at[q], b2_recv.at[y], b2_sem.at[0], b2_sem.at[1], (q * CORES + core, neg)
        ),
    )
    b2_recv[y] = b2_send[y]

    place(2)
    place(3)
    out = pltpu.make_async_copy(rows_acc, rows_hbm, out_sem)
    out.start()

    settle(a2_recv.at[pl.ds(0, NEGS - 1)], a2_sem.at[1])
    a_sum = jnp.sum(a2_recv[...].astype(F32), axis=0)
    settle(b2_recv.at[pl.ds(0, YS - 1)], b2_sem.at[1])
    b_sum = jnp.sum(b2_recv[...].astype(F32), axis=0)
    for j in range(2):
        ngrad_ref[:, j * TILE : (j + 1) * TILE] = a_sum[8 * j : 8 * j + 8]
        ngrad_ref[:, (j + 2) * TILE : (j + 3) * TILE] = b_sum[8 * j : 8 * j + 8]

    settle(ask_send.at[pl.ds(0, REPS - 1)], ask_sem.at[0])
    settle(ask_mid.at[:, pl.ds(0, NEGS - 1)], ask_sem.at[2])
    for k in range(YS):
        settle(row_out.at[k], out_ssem.at[k])
        settle(row_send.at[k, pl.ds(0, NEGS - 1 if k == 0 else NEGS)], row_ssem.at[k])
    settle(emb_all.at[pl.ds(0, NEGS - 1)], emb_sem.at[0])
    settle(sc_all.at[pl.ds(0, NEGS - 1)], sc_sem.at[0])
    settle(eg_send.at[pl.ds(0, NEGS - 1)], eg_sem.at[0])
    for j in range(TILES):
        settle(p_send.at[j], p_ssem.at[j])
    for j in range(2):
        settle(a1_send.at[j, pl.ds(0, YS - 1)], a1_ssem.at[j])
        settle(b1_send.at[j, pl.ds(0, NEGS - 1)], b1_ssem.at[j])
    settle(a2_send.at[pl.ds(0, NEGS - 1)], a2_sem.at[0])
    settle(b2_send.at[pl.ds(0, YS - 1)], b2_sem.at[0])
    out.wait()


def local(
    feature_table, cur_rows, next_owner, next_local, slot_counts, hop_counts, positive_ids,
    neighbor_weight, combine_weight, candidates,
):
    vmem = pl.BlockSpec(memory_space=pltpu.VMEM)
    smem = pl.BlockSpec(memory_space=pltpu.SMEM)
    hbm = pl.BlockSpec(memory_space=pl.ANY)
    dma = pltpu.SemaphoreType.DMA
    part = H // 4
    scratch = [
        pltpu.VMEM((REQ, F), BF16),
        pltpu.VMEM((2, 512, REQ), BF16),
        pltpu.VMEM((F, F), BF16),
        pltpu.VMEM((TILES, F, TILE), BF16),
        pltpu.VMEM((TILES, F + H, TILE), BF16),
        pltpu.VMEM((2 * OWN, H), BF16),
        pltpu.VMEM((TILES, REQ, TILE), BF16),
        pltpu.VMEM((REQ, TILE), BF16),
        pltpu.VMEM((HOP1, F + H), BF16),
        pltpu.VMEM((HOP1, H), F32),
        pltpu.VMEM((HOP1, H), F32),
        pltpu.VMEM((REPS, NEGS, 1, 128), F32),
        pltpu.VMEM((REPS, NEGS, 1, 128), F32),
        pltpu.VMEM((REPS, NEGS, 1, 128), F32),
        pltpu.VMEM((DEVS, 128), F32),
        pltpu.VMEM((YS, NEGS, 16, WIDE), BF16),
        pltpu.VMEM((YS, NEGS, CORES, 16, WIDE), BF16),
        pltpu.VMEM((YS, NEGS, CORES, 16, WIDE), BF16),
        pltpu.VMEM((REQ, F), BF16),
        pltpu.VMEM((REQ, 16), F32),
        pltpu.VMEM((16, part), BF16),
        pltpu.VMEM((NEGS, 16, part), BF16),
        pltpu.VMEM((64, H), BF16),
        pltpu.VMEM((32, 128), F32),
        pltpu.VMEM((NEGS, 32, 128), F32),
        pltpu.VMEM((NEGS, 16, part), BF16),
        pltpu.VMEM((NEGS, 16, part), BF16),
        pltpu.VMEM((TILES, 512, TILE), BF16),
        pltpu.VMEM((TILES, 512, TILE), BF16),
        pltpu.VMEM((TILES, 512, TILE), F32),
        pltpu.VMEM((2, YS, 128, TILE), BF16),
        pltpu.VMEM((2, YS, 128, TILE), BF16),
        pltpu.VMEM((NEGS, 16, TILE), F32),
        pltpu.VMEM((NEGS, 16, TILE), BF16),
        pltpu.VMEM((NEGS, 16, TILE), BF16),
        pltpu.VMEM((NEGS, 32, TILE), F32),
        pltpu.VMEM((2, NEGS, 32, TILE), BF16),
        pltpu.VMEM((2, NEGS, 32, TILE), BF16),
        pltpu.VMEM((YS, 16, TILE), F32),
        pltpu.VMEM((YS, 16, TILE), BF16),
        pltpu.VMEM((YS, 16, TILE), BF16),
        dma((4 + 2 * TILES,)), dma(()),
        dma((4,)), dma((YS,)), dma((YS,)), dma((YS,)), dma((YS,)),
        dma((2,)), dma((2,)), dma((2,)),
        dma((TILES,)), dma((TILES,)),
        dma((2,)), dma((2,)), dma((2,)),
        dma((2,)), dma((2,)), dma((2,)),
    ]
    next_rows, loss, cand_grad, neighbor_grad = pl.pallas_call(
        kernel,
        out_shape=(
            jax.ShapeDtypeStruct((REQ, F), BF16),
            jax.ShapeDtypeStruct((1, B), F32),
            jax.ShapeDtypeStruct((OWN, H), F32),
            jax.ShapeDtypeStruct((8, H), F32),
        ),
        in_specs=[vmem, vmem, vmem, vmem, smem, hbm, hbm, hbm, hbm, hbm],
        out_specs=(hbm, vmem, vmem, vmem),
        scratch_shapes=scratch,
        compiler_params=pltpu.CompilerParams(
            collective_id=0, has_side_effects=True, vmem_limit_bytes=62 * 2**20
        ),
        name="step",
    )(
        next_owner.reshape(1, REQ),
        next_local,
        slot_counts.T,
        hop_counts,
        positive_ids,
        feature_table,
        cur_rows,
        neighbor_weight,
        combine_weight,
        candidates,
    )
    return next_rows, loss.reshape(B), cand_grad, neighbor_grad


def solution(mesh):
    both = P(("rep", "neg"), None)
    flat = P(("rep", "neg"))
    return jax.shard_map(
        local,
        mesh=mesh,
        in_specs=(both, both, both, flat, both, both, flat, P(), P(), both),
        out_specs=(both, flat, both, both),
        check_vma=False,
    )
```

time: 143 us -> 108 us (0.76)
  Pallas kernels: 135 us -> 102 us
  local copies, waits for them, and re-layouts: 6.75 us -> 4.68 us
    pallas_call x1, Pallas kernels: 135 us -> 102 us  [local(): pl.pallas_call(kernel, out_shape=(jax.ShapeDtypeStruct((REQ, F), BF16), j...]
    unnamed x7 -> x10, local copies, waits for them, and re-layouts: 4.13 us -> 4.68 us
where the time goes in v3:
time: 108 us
  Pallas kernels  102 us (94%)
  local copies, waits for them, and re-layouts  4.68 us (4%)
    pallas_call x1, Pallas kernels, local(): pl.pallas_call(kernel, out_shape=(jax.ShapeDtypeStruct((REQ, F), BF16), j...  102 us
    unnamed x10, local copies, waits for them, and re-layouts  4.68 us

profile of v3, /device:TPU:0, one launch (start us, length us, event | category | flops | bytes accessed | tf_op | source)
XLA Modules:
  0.0 107.6 jit_solution(10145621797357958211)
XLA Ops:
  0.6 102.3 %step.1 = (bf16[768,1024]{1,0:T(8,128)(2,1)}, f32[1,4]{1,0:T(1,128)}, f32[64,2048]{1,0:T(8,128)}, f32[8,2048]{1,0:T(8,128)}) custom-call(s32[1,768]{1,0:T(1,128)} %bitcast.4, s32[768]{0:T(1024)} %local_ref.1, s32[16,48]{1,0:T(8,128)} %bitcast.3, s32[4,12]{1,0:T(4,128)} %hop_ref.1, s32[4]{0:T(128)} %pos_ref.1, bf16[1024,1024]{1,0:T(8,128)(2,1)} %table_hbm.1, ...), custom_call_target="tpu_custom_call" | custom-call | tf_op jit(solution)/shard_map/step/pallas_call | solution.py:559
  102.9 0.0 copy-start.2
  102.9 0.0 copy-start
  102.9 0.0 copy-start.1
  102.9 2.7 %copy.18 = bf16[768,1024]{1,0:T(8,128)(2,1)} copy(bf16[768,1024]{1,0:T(8,128)(2,1)} %get-tuple-element.16) | data formatting | bytes 3145728
  105.7 0.0 copy-done.2
  105.7 0.5 copy.19
  106.2 0.0 copy-done
  106.2 0.8 copy.20
  107.0 0.0 copy-done.1
  107.0 0.6 copy.21
Async XLA Ops:
  102.9 2.8 %copy-start.2 = (f32[1,4]{1,0:T(1,128)S(1)}, f32[1,4]{1,0:T(1,128)}, u32[]{:S(2)}) copy-start(f32[1,4]{1,0:T(1,128)} %get-tuple-element.9) | copy-start | bytes 52
  102.9 3.3 %copy-start = (f32[64,2048]{1,0:T(8,128)S(1)}, f32[64,2048]{1,0:T(8,128)}, u32[]{:S(2)}) copy-start(f32[64,2048]{1,0:T(8,128)} %get-tuple-element.18) | copy-start | bytes 1572868
  102.9 4.1 %copy-start.1 = (f32[8,2048]{1,0:T(8,128)S(1)}, f32[8,2048]{1,0:T(8,128)}, u32[]{:S(2)}) copy-start(f32[8,2048]{1,0:T(8,128)} %get-tuple-element.19) | copy-start | bytes 196612

commit v4 on v3

--- a/solution.py
+++ b/solution.py
@@ -50,18 +50,19 @@
 def kernel(
     owner_ref, local_ref, slot_ref, hop_ref, pos_ref,
     table_hbm, cur_hbm, nw_hbm, cw_hbm, cand_hbm,
-    rows_hbm, loss_ref, cand_out, ngrad_ref,
+    rows_acc, loss_ref, cand_out, ngrad_ref,
     cur_v, curt_v, table_v, nw_v, cw_v, cand_v, mask_v, pgrad_v, x_v, mixed_v, pooled_g,
-    ask_send, ask_mid, ask_recv, ids_v, row_out, row_send, row_recv, rows_acc, cols_v,
+    ask_send, ask_mid, ask_recv, ids_v, row_out, row_send, row_recv, cols_v,
     emb_send, emb_all, e_v, sc_send, sc_all, eg_send, eg_recv,
     p_send, p_recv, p_own, a1_send, a1_recv, a2_f, a2_send, a2_recv,
     b1_f, b1_send, b1_recv, b2_f, b2_send, b2_recv,
-    in_sem, out_sem, ask_sem, out_ssem, out_rsem, row_ssem, row_rsem,
+    in_sem, ask_sem, out_ssem, out_rsem, row_ssem, row_rsem,
     emb_sem, sc_sem, eg_sem, p_ssem, p_rsem, a1_ssem, a1_rsem, a2_sem, b1_ssem, b1_rsem, b2_sem,
 ):
     rep = lax.axis_index("rep")
     neg = lax.axis_index("neg")
-    y, core = rep // CORES, rep % CORES
+    y, core = rep // CORES, lax.rem(rep, CORES)
+    x, z = neg // 4, lax.rem(neg, 4)
     mate = (y * CORES + 1 - core, neg)
 
     def send(src, dst, ssem, rsem, where):
@@ -144,7 +145,11 @@
     )
     ask_mid[rep] = ask_send[rep]
 
-    placed = (owner >> 5) * 32 + (owner & 15) * 2 + ((owner >> 4) & 1)
+    from_x = (x + 4 - ((owner >> 2) & 3)) & 3
+    from_z = (z + 4 - (owner & 3)) & 3
+    from_y = (y + 4 - (owner >> 5)) & 3
+    turn = (from_x + from_y + from_z) & 3
+    placed = turn * 32 + (from_x * 4 + from_z) * 2 + ((owner >> 4) & 1)
     eye = bf(iota((REQ, REQ), 0) == iota((REQ, REQ), 1))
     pair = jnp.where(iota((16, REQ), 0) == 0, placed.astype(F32), rank).astype(BF16)
     cols_v[...] = nt(eye, pair)
@@ -182,14 +187,21 @@
     x_v[:, 0:F] = nn(first, cur_v[...]).astype(BF16)
     loads[1].wait()
     settle(ask_recv.at[:, pl.ds(0, NEGS - 1)], ask_sem.at[3])
-    ids_v[...] = ask_recv[...].reshape(DEVS, 128)
-
-    def serve(g):
-        base = pl.multiple_of(g * NEGS, NEGS)
-        asked = ids_v[pl.ds(base, NEGS), :].astype(BF16)
+    line_i, line_d = iota((DEVS, DEVS), 0), iota((DEVS, DEVS), 1)
+    to_x, to_z = (line_i >> 2) & 3, line_i & 3
+    to_y = (y + 8 + (line_i >> 5) - to_x - to_z) & 3
+    target = to_y * 32 + ((line_i >> 4) & 1) * 16 + ((x + to_x) & 3) * 4 + ((z + to_z) & 3)
+    ids_v[...] = nn(bf(target == line_d), ask_recv[...].reshape(DEVS, 128).astype(BF16))
+
+    def serve(k):
+        first_half = pl.multiple_of(k * 32 + (1 - core) * NEGS, NEGS)
+        second_half = pl.multiple_of(k * 32 + core * NEGS, NEGS)
+        asked = jnp.concatenate(
+            [ids_v[pl.ds(first_half, NEGS), :], ids_v[pl.ds(second_half, NEGS), :]], axis=0
+        ).astype(BF16)
 
         def chosen(rows, per, slot_of):
-            wide = nn(bf(iota((rows, NEGS), 0) // per % NEGS == iota((rows, NEGS), 1)), asked)
+            wide = nn(bf(iota((rows, 32), 0) // per % 32 == iota((rows, 32), 1)), asked)
             slot = slot_of(iota((rows, 1), 0))
             at = iota((rows, 128), 1)
             ids = jnp.sum(
@@ -199,46 +211,49 @@
             )
             return bf(ids == iota((rows, F), 1).astype(F32))
 
-        main = nn(chosen(256, 16, lambda r: r % 16), table_v[:, 0:WIDE]).reshape(NEGS, 16, WIDE)
+        main = nn(chosen(512, 16, lambda r: r % 16), table_v[:, 0:WIDE]).reshape(32, 16, WIDE)
         tail = nn(
-            chosen(384, 8, lambda r: jnp.maximum(r % 8 - 4, 0) * 3 + r // 128),
+            chosen(768, 8, lambda r: jnp.maximum(r % 8 - 4, 0) * 3 + r // 256),
             table_v[:, WIDE:F],
         )
-        high = iota((NEGS, 8, PART), 1) >= 4
+        high = iota((32, 8, PART), 1) >= 4
         parts = []
         for c in range(3):
             own = main[:, 8:16, c * PART : (c + 1) * PART]
             parts.append(
-                jnp.where(high, tail[128 * c : 128 * (c + 1)].reshape(NEGS, 8, PART), own)
+                jnp.where(high, tail[256 * c : 256 * (c + 1)].reshape(32, 8, PART), own)
             )
         lower = jnp.concatenate(parts, axis=2)
-        return jnp.concatenate([main[:, 0:8, :], lower], axis=1).astype(BF16)
-
-    def round_of(k):
-        to_y = lax.rem(y + k, YS)
-        row_out[k] = serve(to_y * CORES + 1 - core)
-        send(row_out.at[k], row_send.at[to_y, :, core], out_ssem.at[k], out_rsem.at[k], mate)
-        row_send[to_y, :, core] = serve(to_y * CORES + core)
-        settle(row_out.at[k], out_rsem.at[k])
-
-        def post(n):
-            send(
-                row_send.at[to_y, n], row_recv.at[y, neg], row_ssem.at[k], row_rsem.at[y],
-                (to_y * CORES + core, n),
+        block = jnp.concatenate([main[:, 0:8, :], lower], axis=1).astype(BF16)
+        row_out[k] = block[0:NEGS]
+        send(row_out.at[k], row_send.at[k, :, core], out_ssem.at[k], out_rsem.at[k], mate)
+        row_send[k, :, core] = block[NEGS:32]
+
+    def post(k, part):
+        def one(i, carry):
+            j = lax.rem(i + core * (NEGS - 2 * i), NEGS)
+            dx, dz = j // 4, lax.rem(j, 4)
+            dy = lax.rem(k + 8 - dx - dz, YS)
+            where = (
+                lax.rem(y + dy, YS) * CORES + core,
+                lax.rem(x + dx, 4) * 4 + lax.rem(z + dz, 4),
             )
-
-        around(neg, NEGS, post)
-        if k == 0:
-            row_recv[y, neg] = row_send[y, neg]
-        else:
-            post(neg)
-
-    round_of(0)
-
-    x = x_v[...]
+            send(row_send.at[k, j], row_recv.at[k, j], row_ssem.at[k], row_rsem.at[k], where)
+            return carry
+
+        if part == 0:
+            settle(row_out.at[k], out_rsem.at[k])
+            if k == 0:
+                row_recv[0, 0] = row_send[0, 0]
+        lax.fori_loop(8 * part + (1 if k + part == 0 else 0), 8 * part + 8, one, 0)
+
+    serve(0)
+    post(0, 0)
+
+    pooled_x = x_v[...]
     for j in range(TILES):
         cw_loads[j].wait()
-        mixed_v[:, j * TILE : (j + 1) * TILE] = nn(x, cw_v[j])
+        mixed_v[:, j * TILE : (j + 1) * TILE] = nn(pooled_x, cw_v[j])
     mixed_in = mixed_v[...]
     mixed = jnp.maximum(mixed_in, 0.0)
     inv_mid = lax.rsqrt(jnp.mean(mixed * mixed, axis=1, keepdims=True) + EPSILON)
@@ -266,8 +281,8 @@
     )
     emb_all[neg] = emb_send[...]
 
-    round_of(1)
-
+    post(0, 1)
+    serve(1)
     loads[2].wait()
     loads[3].wait()
     settle(emb_all.at[pl.ds(0, NEGS - 1)], emb_sem.at[1])
@@ -286,9 +301,9 @@
     )
     sc_all[neg] = scores
 
-    round_of(2)
-
-    mates = ids_v[pl.ds(pl.multiple_of(rep * NEGS, NEGS), NEGS), :].astype(BF16)
+    post(1, 0)
+    serve(2)
+    mates = ask_recv[rep].reshape(NEGS, 128).astype(BF16)
     halves = []
     for h in range(2):
         pick = bf(iota((32, NEGS), 0) // B + 8 * h == iota((32, NEGS), 1))
@@ -341,8 +356,7 @@
     )
     eg_recv[neg] = eg_send[neg]
 
-    round_of(3)
-
+    post(1, 1)
     lines = (iota((32, 128), 0) == iota((32, 128), 1) + B * (neg % 8)).astype(F32)
     half = jnp.where(neg // 8 == 0, 0, OWN)
     mine = tn(loss, lines, HIGH)
@@ -364,6 +378,8 @@
         embed_grad.append(nn(move, eg_sum, HIGH))
     embed_grad = jnp.concatenate(embed_grad, axis=1)
 
+    post(2, 0)
+
     top_grad = inv_top * embed_grad - top_in * (
         inv_top * inv_top * inv_top * jnp.mean(embed_grad * top_in, axis=1, keepdims=True)
     )
@@ -388,6 +404,8 @@
         p_send[j] = nn(curt_v[1 - core], pgrad_v[...]).astype(BF16)
         send(p_send.at[j], p_recv.at[j], p_ssem.at[j], p_rsem.at[j], mate)
         p_own[j] = nn(curt_v[core], pgrad_v[...])
+
+    post(2, 1)
 
     for j in order:
         settle(p_recv.at[j], p_rsem.at[j])
@@ -427,11 +445,9 @@
     ]
 
     def place(k):
-        from_y = lax.rem(y - k + YS, YS)
-        got = NEGS - 1 if k == 0 else NEGS
-        settle(row_recv.at[from_y, pl.ds(0, got)], row_rsem.at[from_y])
-        block = row_recv[from_y].reshape(512, WIDE)
-        line = (iota((REQ, 512), 1) + from_y * 512).astype(F32)
+        settle(row_recv.at[k, pl.ds(0, NEGS - 1 if k == 0 else NEGS)], row_rsem.at[k])
+        block = row_recv[k].reshape(512, WIDE)
+        line = (iota((REQ, 512), 1) + k * 512).astype(F32)
         body = nn(bf(line == slot_main), block)
         tail = jnp.zeros((REQ, PART), F32)
         for c in range(3):
@@ -439,6 +455,8 @@
         new = jnp.concatenate([body, tail], axis=1).astype(BF16)
         rows_acc[...] = new if k == 0 else rows_acc[...] + new
 
+    serve(3)
+    post(3, 0)
     place(0)
     place(1)
 
@@ -467,11 +485,9 @@
     )
     b2_recv[y] = b2_send[y]
 
+    post(3, 1)
     place(2)
     place(3)
-    out = pltpu.make_async_copy(rows_acc, rows_hbm, out_sem)
-    out.start()
-
     settle(a2_recv.at[pl.ds(0, NEGS - 1)], a2_sem.at[1])
     a_sum = jnp.sum(a2_recv[...].astype(F32), axis=0)
     settle(b2_recv.at[pl.ds(0, YS - 1)], b2_sem.at[1])
@@ -495,7 +511,6 @@
         settle(b1_send.at[j, pl.ds(0, NEGS - 1)], b1_ssem.at[j])
     settle(a2_send.at[pl.ds(0, NEGS - 1)], a2_sem.at[0])
     settle(b2_send.at[pl.ds(0, YS - 1)], b2_sem.at[0])
-    out.wait()
 
 
 def local(
@@ -526,7 +541,6 @@
         pltpu.VMEM((YS, NEGS, 16, WIDE), BF16),
         pltpu.VMEM((YS, NEGS, CORES, 16, WIDE), BF16),
         pltpu.VMEM((YS, NEGS, CORES, 16, WIDE), BF16),
-        pltpu.VMEM((REQ, F), BF16),
         pltpu.VMEM((REQ, 16), F32),
         pltpu.VMEM((16, part), BF16),
         pltpu.VMEM((NEGS, 16, part), BF16),
@@ -549,7 +563,7 @@
         pltpu.VMEM((YS, 16, TILE), F32),
         pltpu.VMEM((YS, 16, TILE), BF16),
         pltpu.VMEM((YS, 16, TILE), BF16),
-        dma((4 + 2 * TILES,)), dma(()),
+        dma((4 + 2 * TILES,)),
         dma((4,)), dma((YS,)), dma((YS,)), dma((YS,)), dma((YS,)),
         dma((2,)), dma((2,)), dma((2,)),
         dma((TILES,)), dma((TILES,)),
@@ -559,16 +573,16 @@
     next_rows, loss, cand_grad, neighbor_grad = pl.pallas_call(
         kernel,
         out_shape=(
-            jax.ShapeDtypeStruct((REQ, F), BF16),
-            jax.ShapeDtypeStruct((1, B), F32),
-            jax.ShapeDtypeStruct((OWN, H), F32),
-            jax.ShapeDtypeStruct((8, H), F32),
+            pltpu.VMEM((REQ, F), BF16),
+            pltpu.VMEM((1, B), F32),
+            pltpu.VMEM((OWN, H), F32),
+            pltpu.VMEM((8, H), F32),
         ),
         in_specs=[vmem, vmem, vmem, vmem, smem, hbm, hbm, hbm, hbm, hbm],
-        out_specs=(hbm, vmem, vmem, vmem),
+        out_specs=(vmem, vmem, vmem, vmem),
         scratch_shapes=scratch,
         compiler_params=pltpu.CompilerParams(
-            collective_id=0, has_side_effects=True, vmem_limit_bytes=62 * 2**20
+            collective_id=0, has_side_effects=True, vmem_limit_bytes=58 * 2**20
         ),
         name="step",
     )(

time: 108 us -> 98 us (0.907)
  Pallas kernels: 102 us -> 93 us
  local copies, waits for them, and re-layouts: 4.68 us -> 3.08 us
    pallas_call x1, Pallas kernels: 102 us -> 93 us  [local(): pl.pallas_call(kernel, out_shape=(pltpu.VMEM((REQ, F), BF16), pltpu.VMEM(...]
    unnamed x10 -> x4, local copies, waits for them, and re-layouts: 4.68 us -> 3.08 us
where the time goes in v4:
time: 98 us; the launch traced here: 96.7 us
  Pallas kernels  93 us (95%)
  local copies, waits for them, and re-layouts  3.08 us (3%)
    pallas_call x1, Pallas kernels, local(): pl.pallas_call(kernel, out_shape=(pltpu.VMEM((REQ, F), BF16), pltpu.VMEM(...  93 us
    unnamed x4, local copies, waits for them, and re-layouts  3.08 us

profile of v4, /device:TPU:0, one launch (start us, length us, event | category | flops | bytes accessed | tf_op | source)
XLA Modules:
  0.0 96.7 jit_solution(18073400943339554653)
XLA Ops:
  0.6 93.0 %step.1 = (bf16[768,1024]{1,0:T(8,128)(2,1)S(1)}, f32[1,4]{1,0:T(1,128)S(1)}, f32[64,2048]{1,0:T(8,128)S(1)}, f32[8,2048]{1,0:T(8,128)S(1)}) custom-call(s32[1,768]{1,0:T(1,128)} %bitcast.5, s32[768]{0:T(1024)} %local_ref.1, s32[16,48]{1,0:T(8,128)} %bitcast.4, s32[4,12]{1,0:T(4,128)} %hop_ref.1, s32[4]{0:T(128)} %pos_ref.1, bf16[1024,1024]{1,0:T(8,128)(2,1)} %table_hbm.1, ...), custom_call_target="tpu_custom_call" | custom-call | tf_op jit(solution)/shard_map/step/pallas_call | solution.py:573
  93.6 1.1 %copy.18 = bf16[768,1024]{1,0:T(8,128)(2,1)} copy(bf16[768,1024]{1,0:T(8,128)(2,1)S(1)} %get-tuple-element.12) | data formatting | bytes 3145728
  94.8 0.5 copy.19
  95.3 0.6 copy.21
  95.9 0.8 copy.20

commit v5 on v4

--- a/solution.py
+++ b/solution.py
@@ -21,6 +21,9 @@
 PART = 256
 WIDE = 3 * PART
 OWN = 64
+COLS = ((0, 768), (768, 1408), (1408, 2048))
+ORDERS = ((0, 1, 2), (1, 2, 0), (2, 0, 1))
+STOPS = (16, 28, 40, 52, 60, 64, 64, 64)
 
 
 def iota(shape, dim):
@@ -54,10 +57,9 @@
     cur_v, curt_v, table_v, nw_v, cw_v, cand_v, mask_v, pgrad_v, x_v, mixed_v, pooled_g,
     ask_send, ask_mid, ask_recv, ids_v, row_out, row_send, row_recv, cols_v,
     emb_send, emb_all, e_v, sc_send, sc_all, eg_send, eg_recv,
-    p_send, p_recv, p_own, a1_send, a1_recv, a2_f, a2_send, a2_recv,
-    b1_f, b1_send, b1_recv, b2_f, b2_send, b2_recv,
+    p_send, p_recv, p_own, s1_send, s1_recv, s2_send, s2_recv, s3_send, s3_recv,
     in_sem, ask_sem, out_ssem, out_rsem, row_ssem, row_rsem,
-    emb_sem, sc_sem, eg_sem, p_ssem, p_rsem, a1_ssem, a1_rsem, a2_sem, b1_ssem, b1_rsem, b2_sem,
+    emb_sem, sc_sem, eg_sem, p_ssem, p_rsem, s_ssem, s_rsem,
 ):
     rep = lax.axis_index("rep")
     neg = lax.axis_index("neg")
@@ -80,6 +82,14 @@
             return carry
 
         lax.fori_loop(1, count, step, 0)
+
+    barrier = pltpu.get_barrier_semaphore()
+
+    def greet(where):
+        pl.semaphore_signal(barrier, inc=1, device_id=where, device_id_type=MESH)
+
+    around(neg, NEGS, lambda n: greet((rep, n)))
+    around(rep, REPS, lambda r: greet((r, neg)))
 
     loads = [
         pltpu.make_async_copy(cur_hbm, cur_v, in_sem.at[0]),
@@ -107,14 +117,6 @@
     for load in cw_loads:
         load.start()
 
-    barrier = pltpu.get_barrier_semaphore()
-
-    def greet(where):
-        pl.semaphore_signal(barrier, inc=1, device_id=where, device_id_type=MESH)
-
-    around(neg, NEGS, lambda n: greet((rep, n)))
-    around(rep, REPS, lambda r: greet((r, neg)))
-
     owner = owner_ref[...]
     hit = owner == iota((DEVS, REQ), 0)
     hit_low = bf(hit)
@@ -166,13 +168,11 @@
     def project(j):
         nw_loads[j].wait()
         projected = nn(cur_v[...], nw_v[j])
-        mask_v[j] = bf(projected > 0.0)
+        mask_v[:, j * TILE : (j + 1) * TILE] = bf(projected > 0.0)
         weighted = jnp.maximum(projected, 0.0) * weight
         pooled = jnp.sum(weighted.reshape(HOP1, SLOTS, TILE), axis=1)
         x_v[:, F + j * TILE : F + (j + 1) * TILE] = pooled.astype(BF16)
 
-    for j in range(TILES // 2):
-        project(j)
     settle(ask_mid.at[pl.ds(0, REPS - 1)], ask_sem.at[1])
     around(
         neg, NEGS,
@@ -181,10 +181,8 @@
         ),
     )
     ask_recv[:, neg] = ask_mid[:, neg]
-    for j in range(TILES // 2, TILES):
+    for j in range(TILES // 2):
         project(j)
-    first = bf(iota((HOP1, REQ), 0) * SLOTS == iota((HOP1, REQ), 1))
-    x_v[:, 0:F] = nn(first, cur_v[...]).astype(BF16)
     loads[1].wait()
     settle(ask_recv.at[:, pl.ds(0, NEGS - 1)], ask_sem.at[3])
     line_i, line_d = iota((DEVS, DEVS), 0), iota((DEVS, DEVS), 1)
@@ -229,26 +227,46 @@
         send(row_out.at[k], row_send.at[k, :, core], out_ssem.at[k], out_rsem.at[k], mate)
         row_send[k, :, core] = block[NEGS:32]
 
-    def post(k, part):
-        def one(i, carry):
-            j = lax.rem(i + core * (NEGS - 2 * i), NEGS)
-            dx, dz = j // 4, lax.rem(j, 4)
-            dy = lax.rem(k + 8 - dx - dz, YS)
-            where = (
-                lax.rem(y + dy, YS) * CORES + core,
-                lax.rem(x + dx, 4) * 4 + lax.rem(z + dz, 4),
-            )
-            send(row_send.at[k, j], row_recv.at[k, j], row_ssem.at[k], row_rsem.at[k], where)
-            return carry
-
-        if part == 0:
-            settle(row_out.at[k], out_rsem.at[k])
-            if k == 0:
-                row_recv[0, 0] = row_send[0, 0]
-        lax.fori_loop(8 * part + (1 if k + part == 0 else 0), 8 * part + 8, one, 0)
-
-    serve(0)
-    post(0, 0)
+    done = {"sent": 0, "served": 0}
+
+    def serve_to(rounds):
+        while done["served"] < rounds:
+            serve(done["served"])
+            done["served"] += 1
+
+    def post_to(limit, rounds=0):
+        while done["sent"] < limit:
+            k = done["sent"] // NEGS
+            serve_to(k + 1)
+            low, high = done["sent"] - k * NEGS, min(limit - k * NEGS, NEGS)
+            done["sent"] = k * NEGS + high
+
+            def one(i, carry):
+                j = lax.rem(i + core * (NEGS - 2 * i), NEGS)
+                dx, dz = j // 4, lax.rem(j, 4)
+                dy = lax.rem(k + 8 - dx - dz, YS)
+                where = (
+                    lax.rem(y + dy, YS) * CORES + core,
+                    lax.rem(x + dx, 4) * 4 + lax.rem(z + dz, 4),
+                )
+                send(
+                    row_send.at[k, j], row_recv.at[k, j], row_ssem.at[k], row_rsem.at[k], where
+                )
+                return carry
+
+            if low == 0:
+                settle(row_out.at[k], out_rsem.at[k])
+                if k == 0:
+                    row_recv[0, 0] = row_send[0, 0]
+                    low = 1
+            lax.fori_loop(low, high, one, 0)
+        serve_to(rounds)
+
+    post_to(STOPS[0], 1)
+    for j in range(TILES // 2, TILES):
+        project(j)
+    first = bf(iota((HOP1, REQ), 0) * SLOTS == iota((HOP1, REQ), 1))
+    x_v[:, 0:F] = nn(first, cur_v[...]).astype(BF16)
 
     pooled_x = x_v[...]
     for j in range(TILES):
@@ -281,8 +299,7 @@
     )
     emb_all[neg] = emb_send[...]
 
-    post(0, 1)
-    serve(1)
+    post_to(STOPS[1], 2)
     loads[2].wait()
     loads[3].wait()
     settle(emb_all.at[pl.ds(0, NEGS - 1)], emb_sem.at[1])
@@ -301,8 +318,7 @@
     )
     sc_all[neg] = scores
 
-    post(1, 0)
-    serve(2)
+    post_to(STOPS[2], 3)
     mates = ask_recv[rep].reshape(NEGS, 128).astype(BF16)
     halves = []
     for h in range(2):
@@ -356,18 +372,20 @@
     )
     eg_recv[neg] = eg_send[neg]
 
-    post(1, 1)
-    lines = (iota((32, 128), 0) == iota((32, 128), 1) + B * (neg % 8)).astype(F32)
-    half = jnp.where(neg // 8 == 0, 0, OWN)
-    mine = tn(loss, lines, HIGH)
-    loss_ref[...] = jnp.sum(
-        jnp.where(iota((128, 128), 0) == half, mine, 0.0), axis=0, keepdims=True
-    )[:, 0:B]
-    cand_out[...] = tn(g_left, e_v[0:32, :])[0:OWN] + tn(g_right, e_v[32:64, :])[OWN:128]
+    post_to(STOPS[3], 4)
     for b in range(8):
-        curt_v[b % 2, 128 * (b // 2) : 128 * (b // 2) + 128, :] = (
+        curt_v[0, b % 2, 128 * (b // 2) : 128 * (b // 2) + 128, :] = (
             cur_v[:, 128 * b : 128 * b + 128].astype(F32).T.astype(BF16)
         )
+    r, source = iota((512, 512), 0), iota((512, 512), 1)
+    high, middle, low = r >> 7, (r >> 5) & 3, (r >> 3) & 3
+    for t, rows_from in (
+        (1, low * 128 + high * 32 + middle * 8 + (r & 7)),
+        (2, middle * 128 + low * 32 + high * 8 + (r & 7)),
+    ):
+        move = bf(rows_from == source)
+        for c in range(CORES):
+            curt_v[t, c] = nn(move, curt_v[0, c]).astype(BF16)
     settle(eg_recv.at[pl.ds(0, NEGS - 1)], eg_sem.at[1])
     eg_sum = jnp.sum(eg_recv[...].astype(F32), axis=0)
     embed_grad = []
@@ -378,7 +396,7 @@
         embed_grad.append(nn(move, eg_sum, HIGH))
     embed_grad = jnp.concatenate(embed_grad, axis=1)
 
-    post(2, 0)
+    post_to(STOPS[4])
 
     top_grad = inv_top * embed_grad - top_in * (
         inv_top * inv_top * inv_top * jnp.mean(embed_grad * top_in, axis=1, keepdims=True)
@@ -393,47 +411,67 @@
         total = total + nt(mixed_in_grad[:, j * TILE : (j + 1) * TILE], cw_v[j, F : F + H, :])
     pooled_g[...] = total
 
-    order = (0, 2, 1, 3)
-    for j in order:
+    post_to(STOPS[5])
+
+    def products(t, slot):
+        low, high = COLS[t]
+        width = high - low
         spread_grad = jnp.broadcast_to(
-            pooled_g[:, j * TILE : (j + 1) * TILE][:, None, :], (HOP1, SLOTS, TILE)
-        ).reshape(REQ, TILE)
-        pgrad_v[...] = jnp.where(mask_v[j].astype(F32) > 0.0, spread_grad * weight, 0.0).astype(
-            BF16
+            pooled_g[:, low:high][:, None, :], (HOP1, SLOTS, width)
+        ).reshape(REQ, width)
+        pgrad_v[slot, :, 0:width] = jnp.where(
+            mask_v[:, low:high].astype(F32) > 0.0, spread_grad * weight, 0.0
+        ).astype(BF16)
+        p_send[:, low:high] = nn(curt_v[t, 1 - core], pgrad_v[slot, :, 0:width]).astype(BF16)
+        cols = pl.ds(low, width)
+        send(p_send.at[:, cols], p_recv.at[:, cols], p_ssem.at[t], p_rsem.at[t], mate)
+        p_own[slot, :, 0:width] = nn(curt_v[t, core], pgrad_v[slot, :, 0:width])
+
+    here = (y, x, z)
+
+    def along(axis, body):
+        def one(q):
+            where = ((q * CORES + core, neg), (rep, q * 4 + z), (rep, x * 4 + q))[axis]
+            body(q, where)
+
+        around(here[axis], YS, one)
+
+    stages = ((s1_send, s1_recv), (s2_send, s2_recv), (s3_send, s3_recv))
+
+    def scatter(t, stage, total):
+        low, high = COLS[t]
+        width, axis = high - low, ORDERS[t][stage]
+        out, back = stages[stage]
+        cols = pl.ds(0, width)
+        rows = out.shape[2]
+        out[t, :, :, 0:width] = total.astype(out.dtype).reshape(YS, rows, width)
+        along(
+            axis,
+            lambda q, where: send(
+                out.at[t, q, :, cols], back.at[t, here[axis], :, cols],
+                s_ssem.at[stage, t], s_rsem.at[stage, t], where,
+            ),
         )
-        p_send[j] = nn(curt_v[1 - core], pgrad_v[...]).astype(BF16)
-        send(p_send.at[j], p_recv.at[j], p_ssem.at[j], p_rsem.at[j], mate)
-        p_own[j] = nn(curt_v[core], pgrad_v[...])
-
-    post(2, 1)
-
-    for j in order:
-        settle(p_recv.at[j], p_rsem.at[j])
-        chip_sum = p_own[j] + p_recv[j].astype(F32)
-        if j < 2:
-            a1_send[j] = chip_sum.astype(BF16).reshape(YS, 128, TILE)
-            around(
-                y, YS,
-                lambda q, j=j: send(
-                    a1_send.at[j, q], a1_recv.at[j, y], a1_ssem.at[j], a1_rsem.at[j],
-                    (q * CORES + core, neg),
-                ),
-            )
-            a1_recv[j, y] = a1_send[j, y]
-        else:
-            k = j - 2
-            for q in range(YS):
-                b1_f[:, 8 * q : 8 * q + 8, :] = chip_sum[128 * q : 128 * q + 128].reshape(
-                    NEGS, 8, TILE
-                )
-            b1_send[k] = b1_f[...].astype(BF16)
-            around(
-                neg, NEGS,
-                lambda n, k=k: send(
-                    b1_send.at[k, n], b1_recv.at[k, neg], b1_ssem.at[k], b1_rsem.at[k], (rep, n)
-                ),
-            )
-            b1_recv[k, neg] = b1_send[k, neg]
+        back[t, here[axis], :, 0:width] = out[t, here[axis], :, 0:width]
+
+    def gather(t, stage):
+        low, high = COLS[t]
+        width = high - low
+        back = stages[stage][1]
+        settle(back.at[t, pl.ds(0, YS - 1), :, pl.ds(0, width)], s_rsem.at[stage, t])
+        return jnp.sum(back[t, :, :, 0:width].astype(F32), axis=0)
+
+    def pass_on(t, slot):
+        low, high = COLS[t]
+        settle(p_recv.at[:, pl.ds(low, high - low)], p_rsem.at[t])
+        scatter(t, 0, p_own[slot, :, 0 : high - low] + p_recv[:, low:high].astype(F32))
+
+    for t in range(3):
+        products(t, t % 2)
+        if t > 0:
+            pass_on(t - 1, (t - 1) % 2)
+    pass_on(2, 0)
+    post_to(STOPS[6])
 
     owner_col = cols_v[:, 0:1]
     rank_col = cols_v[:, 1:2]
@@ -455,46 +493,25 @@
         new = jnp.concatenate([body, tail], axis=1).astype(BF16)
         rows_acc[...] = new if k == 0 else rows_acc[...] + new
 
-    serve(3)
-    post(3, 0)
+    lines = (iota((32, 128), 0) == iota((32, 128), 1) + B * (neg % 8)).astype(F32)
+    half = jnp.where(neg // 8 == 0, 0, OWN)
+    mine = tn(loss, lines, HIGH)
+    loss_ref[...] = jnp.sum(
+        jnp.where(iota((128, 128), 0) == half, mine, 0.0), axis=0, keepdims=True
+    )[:, 0:B]
+    cand_out[...] = tn(g_left, e_v[0:32, :])[0:OWN] + tn(g_right, e_v[32:64, :])[OWN:128]
     place(0)
+
+    for t in range(3):
+        scatter(t, 1, gather(t, 0))
+    post_to(STOPS[7])
     place(1)
-
-    for j in range(2):
-        settle(a1_recv.at[j, pl.ds(0, YS - 1)], a1_rsem.at[j])
-        a2_f[:, 8 * j : 8 * j + 8, :] = jnp.sum(a1_recv[j].astype(F32), axis=0).reshape(
-            NEGS, 8, TILE
-        )
-    a2_send[...] = a2_f[...].astype(BF16)
-    around(
-        neg, NEGS,
-        lambda n: send(a2_send.at[n], a2_recv.at[neg], a2_sem.at[0], a2_sem.at[1], (rep, n)),
-    )
-    a2_recv[neg] = a2_send[neg]
-    for k in range(2):
-        settle(b1_recv.at[k, pl.ds(0, NEGS - 1)], b1_rsem.at[k])
-        b2_f[:, 8 * k : 8 * k + 8, :] = jnp.sum(b1_recv[k].astype(F32), axis=0).reshape(
-            YS, 8, TILE
-        )
-    b2_send[...] = b2_f[...].astype(BF16)
-    around(
-        y, YS,
-        lambda q: send(
-            b2_send.at[q], b2_recv.at[y], b2_sem.at[0], b2_sem.at[1], (q * CORES + core, neg)
-        ),
-    )
-    b2_recv[y] = b2_send[y]
-
-    post(3, 1)
+    for t in range(3):
+        scatter(t, 2, gather(t, 1))
     place(2)
+    for t in range(3):
+        ngrad_ref[:, COLS[t][0] : COLS[t][1]] = gather(t, 2)
     place(3)
-    settle(a2_recv.at[pl.ds(0, NEGS - 1)], a2_sem.at[1])
-    a_sum = jnp.sum(a2_recv[...].astype(F32), axis=0)
-    settle(b2_recv.at[pl.ds(0, YS - 1)], b2_sem.at[1])
-    b_sum = jnp.sum(b2_recv[...].astype(F32), axis=0)
-    for j in range(2):
-        ngrad_ref[:, j * TILE : (j + 1) * TILE] = a_sum[8 * j : 8 * j + 8]
-        ngrad_ref[:, (j + 2) * TILE : (j + 3) * TILE] = b_sum[8 * j : 8 * j + 8]
 
     settle(ask_send.at[pl.ds(0, REPS - 1)], ask_sem.at[0])
     settle(ask_mid.at[:, pl.ds(0, NEGS - 1)], ask_sem.at[2])
@@ -504,13 +521,13 @@
     settle(emb_all.at[pl.ds(0, NEGS - 1)], emb_sem.at[0])
     settle(sc_all.at[pl.ds(0, NEGS - 1)], sc_sem.at[0])
     settle(eg_send.at[pl.ds(0, NEGS - 1)], eg_sem.at[0])
-    for j in range(TILES):
-        settle(p_send.at[j], p_ssem.at[j])
-    for j in range(2):
-        settle(a1_send.at[j, pl.ds(0, YS - 1)], a1_ssem.at[j])
-        settle(b1_send.at[j, pl.ds(0, NEGS - 1)], b1_ssem.at[j])
-    settle(a2_send.at[pl.ds(0, NEGS - 1)], a2_sem.at[0])
-    settle(b2_send.at[pl.ds(0, YS - 1)], b2_sem.at[0])
+    for t, (low, high) in enumerate(COLS):
+        settle(p_send.at[:, pl.ds(low, high - low)], p_ssem.at[t])
+        for stage in range(3):
+            settle(
+                stages[stage][0].at[t, pl.ds(0, YS - 1), :, pl.ds(0, high - low)],
+                s_ssem.at[stage, t],
+            )
 
 
 def local(
@@ -524,13 +541,13 @@
     part = H // 4
     scratch = [
         pltpu.VMEM((REQ, F), BF16),
-        pltpu.VMEM((2, 512, REQ), BF16),
+        pltpu.VMEM((3, 2, 512, REQ), BF16),
         pltpu.VMEM((F, F), BF16),
         pltpu.VMEM((TILES, F, TILE), BF16),
         pltpu.VMEM((TILES, F + H, TILE), BF16),
         pltpu.VMEM((2 * OWN, H), BF16),
-        pltpu.VMEM((TILES, REQ, TILE), BF16),
-        pltpu.VMEM((REQ, TILE), BF16),
+        pltpu.VMEM((REQ, H), BF16),
+        pltpu.VMEM((2, REQ, 768), BF16),
         pltpu.VMEM((HOP1, F + H), BF16),
         pltpu.VMEM((HOP1, H), F32),
         pltpu.VMEM((HOP1, H), F32),
@@ -549,26 +566,20 @@
         pltpu.VMEM((NEGS, 32, 128), F32),
         pltpu.VMEM((NEGS, 16, part), BF16),
         pltpu.VMEM((NEGS, 16, part), BF16),
-        pltpu.VMEM((TILES, 512, TILE), BF16),
-        pltpu.VMEM((TILES, 512, TILE), BF16),
-        pltpu.VMEM((TILES, 512, TILE), F32),
-        pltpu.VMEM((2, YS, 128, TILE), BF16),
-        pltpu.VMEM((2, YS, 128, TILE), BF16),
-        pltpu.VMEM((NEGS, 16, TILE), F32),
-        pltpu.VMEM((NEGS, 16, TILE), BF16),
-        pltpu.VMEM((NEGS, 16, TILE), BF16),
-        pltpu.VMEM((NEGS, 32, TILE), F32),
-        pltpu.VMEM((2, NEGS, 32, TILE), BF16),
-        pltpu.VMEM((2, NEGS, 32, TILE), BF16),
-        pltpu.VMEM((YS, 16, TILE), F32),
-        pltpu.VMEM((YS, 16, TILE), BF16),
-        pltpu.VMEM((YS, 16, TILE), BF16),
+        pltpu.VMEM((512, H), BF16),
+        pltpu.VMEM((512, H), BF16),
+        pltpu.VMEM((2, 512, 768), F32),
+        pltpu.VMEM((3, YS, 128, 768), BF16),
+        pltpu.VMEM((3, YS, 128, 768), BF16),
+        pltpu.VMEM((3, YS, 32, 768), BF16),
+        pltpu.VMEM((3, YS, 32, 768), BF16),
+        pltpu.VMEM((3, YS, 8, 768), F32),
+        pltpu.VMEM((3, YS, 8, 768), F32),
         dma((4 + 2 * TILES,)),
         dma((4,)), dma((YS,)), dma((YS,)), dma((YS,)), dma((YS,)),
         dma((2,)), dma((2,)), dma((2,)),
-        dma((TILES,)), dma((TILES,)),
-        dma((2,)), dma((2,)), dma((2,)),
-        dma((2,)), dma((2,)), dma((2,)),
+        dma((3,)), dma((3,)),
+        dma((3, 3)), dma((3, 3)),
     ]
     next_rows, loss, cand_grad, neighbor_grad = pl.pallas_call(
         kernel,
@@ -582,7 +593,7 @@
         out_specs=(vmem, vmem, vmem, vmem),
         scratch_shapes=scratch,
         compiler_params=pltpu.CompilerParams(
-            collective_id=0, has_side_effects=True, vmem_limit_bytes=58 * 2**20
+            collective_id=0, has_side_effects=True, vmem_limit_bytes=60 * 2**20
         ),
         name="step",
     )(

time: 98 us -> 99.9 us (1.019); the launches traced: 96.7 us -> 99.8 us
  Pallas kernels: 93 us -> 96 us
    pallas_call x1, Pallas kernels: 93 us -> 96 us  [local(): pl.pallas_call(kernel, out_shape=(pltpu.VMEM((REQ, F), BF16), pltpu.VMEM(...]
where the time goes in v5:
time: 99.9 us; the launch traced here: 99.8 us
  Pallas kernels  96 us (96%)
  local copies, waits for them, and re-layouts  3.08 us (3%)
    pallas_call x1, Pallas kernels, local(): pl.pallas_call(kernel, out_shape=(pltpu.VMEM((REQ, F), BF16), pltpu.VMEM(...  96 us
    unnamed x4, local copies, waits for them, and re-layouts  3.08 us

profile of v5, /device:TPU:0, one launch (start us, length us, event | category | flops | bytes accessed | tf_op | source)
XLA Modules:
  0.0 99.8 jit_solution(10896286817204088925)
XLA Ops:
  0.6 96.0 %step.1 = (bf16[768,1024]{1,0:T(8,128)(2,1)S(1)}, f32[1,4]{1,0:T(1,128)S(1)}, f32[64,2048]{1,0:T(8,128)S(1)}, f32[8,2048]{1,0:T(8,128)S(1)}) custom-call(s32[1,768]{1,0:T(1,128)} %bitcast.5, s32[768]{0:T(1024)} %local_ref.1, s32[16,48]{1,0:T(8,128)} %bitcast.4, s32[4,12]{1,0:T(4,128)} %hop_ref.1, s32[4]{0:T(128)} %pos_ref.1, bf16[1024,1024]{1,0:T(8,128)(2,1)} %table_hbm.1, ...), custom_call_target="tpu_custom_call" | custom-call | tf_op jit(solution)/shard_map/step/pallas_call | solution.py:584
  96.7 1.1 %copy.18 = bf16[768,1024]{1,0:T(8,128)(2,1)} copy(bf16[768,1024]{1,0:T(8,128)(2,1)S(1)} %get-tuple-element.12) | data formatting | bytes 3145728
  97.8 0.5 copy.19
  98.3 0.6 copy.21
  99.0 0.8 copy.20

commit v6 on v4

--- a/solution.py
+++ b/solution.py
@@ -21,6 +21,7 @@
 PART = 256
 WIDE = 3 * PART
 OWN = 64
+STOPS = (16, 26, 38, 50, 58, 64, 64, 64)
 
 
 def iota(shape, dim):
@@ -81,6 +82,14 @@
 
         lax.fori_loop(1, count, step, 0)
 
+    barrier = pltpu.get_barrier_semaphore()
+
+    def greet(where):
+        pl.semaphore_signal(barrier, inc=1, device_id=where, device_id_type=MESH)
+
+    around(neg, NEGS, lambda n: greet((rep, n)))
+    around(rep, REPS, lambda r: greet((r, neg)))
+
     loads = [
         pltpu.make_async_copy(cur_hbm, cur_v, in_sem.at[0]),
         pltpu.make_async_copy(table_hbm, table_v, in_sem.at[1]),
@@ -102,18 +111,6 @@
     loads[0].start()
     for load in nw_loads:
         load.start()
-    for load in loads[1:]:
-        load.start()
-    for load in cw_loads:
-        load.start()
-
-    barrier = pltpu.get_barrier_semaphore()
-
-    def greet(where):
-        pl.semaphore_signal(barrier, inc=1, device_id=where, device_id_type=MESH)
-
-    around(neg, NEGS, lambda n: greet((rep, n)))
-    around(rep, REPS, lambda r: greet((r, neg)))
 
     owner = owner_ref[...]
     hit = owner == iota((DEVS, REQ), 0)
@@ -144,6 +141,10 @@
         ),
     )
     ask_mid[rep] = ask_send[rep]
+    for load in loads[1:]:
+        load.start()
+    for load in cw_loads:
+        load.start()
 
     from_x = (x + 4 - ((owner >> 2) & 3)) & 3
     from_z = (z + 4 - (owner & 3)) & 3
@@ -171,8 +172,6 @@
         pooled = jnp.sum(weighted.reshape(HOP1, SLOTS, TILE), axis=1)
         x_v[:, F + j * TILE : F + (j + 1) * TILE] = pooled.astype(BF16)
 
-    for j in range(TILES // 2):
-        project(j)
     settle(ask_mid.at[pl.ds(0, REPS - 1)], ask_sem.at[1])
     around(
         neg, NEGS,
@@ -181,10 +180,8 @@
         ),
     )
     ask_recv[:, neg] = ask_mid[:, neg]
-    for j in range(TILES // 2, TILES):
+    for j in range(TILES // 2):
         project(j)
-    first = bf(iota((HOP1, REQ), 0) * SLOTS == iota((HOP1, REQ), 1))
-    x_v[:, 0:F] = nn(first, cur_v[...]).astype(BF16)
     loads[1].wait()
     settle(ask_recv.at[:, pl.ds(0, NEGS - 1)], ask_sem.at[3])
     line_i, line_d = iota((DEVS, DEVS), 0), iota((DEVS, DEVS), 1)
@@ -229,26 +226,46 @@
         send(row_out.at[k], row_send.at[k, :, core], out_ssem.at[k], out_rsem.at[k], mate)
         row_send[k, :, core] = block[NEGS:32]
 
-    def post(k, part):
-        def one(i, carry):
-            j = lax.rem(i + core * (NEGS - 2 * i), NEGS)
-            dx, dz = j // 4, lax.rem(j, 4)
-            dy = lax.rem(k + 8 - dx - dz, YS)
-            where = (
-                lax.rem(y + dy, YS) * CORES + core,
-                lax.rem(x + dx, 4) * 4 + lax.rem(z + dz, 4),
-            )
-            send(row_send.at[k, j], row_recv.at[k, j], row_ssem.at[k], row_rsem.at[k], where)
-            return carry
-
-        if part == 0:
-            settle(row_out.at[k], out_rsem.at[k])
-            if k == 0:
-                row_recv[0, 0] = row_send[0, 0]
-        lax.fori_loop(8 * part + (1 if k + part == 0 else 0), 8 * part + 8, one, 0)
-
-    serve(0)
-    post(0, 0)
+    done = {"sent": 0, "served": 0}
+
+    def serve_to(rounds):
+        while done["served"] < rounds:
+            serve(done["served"])
+            done["served"] += 1
+
+    def post_to(limit, rounds=0):
+        while done["sent"] < limit:
+            k = done["sent"] // NEGS
+            serve_to(k + 1)
+            low, high = done["sent"] - k * NEGS, min(limit - k * NEGS, NEGS)
+            done["sent"] = k * NEGS + high
+
+            def one(i, carry):
+                j = lax.rem(i + core * (NEGS - 2 * i), NEGS)
+                dx, dz = j // 4, lax.rem(j, 4)
+                dy = lax.rem(k + 8 - dx - dz, YS)
+                where = (
+                    lax.rem(y + dy, YS) * CORES + core,
+                    lax.rem(x + dx, 4) * 4 + lax.rem(z + dz, 4),
+                )
+                send(
+                    row_send.at[k, j], row_recv.at[k, j], row_ssem.at[k], row_rsem.at[k], where
+                )
+                return carry
+
+            if low == 0:
+                settle(row_out.at[k], out_rsem.at[k])
+                if k == 0:
+                    row_recv[0, 0] = row_send[0, 0]
+                    low = 1
+            lax.fori_loop(low, high, one, 0)
+        serve_to(rounds)
+
+    post_to(STOPS[0], 1)
+    for j in range(TILES // 2, TILES):
+        project(j)
+    first = bf(iota((HOP1, REQ), 0) * SLOTS == iota((HOP1, REQ), 1))
+    x_v[:, 0:F] = nn(first, cur_v[...]).astype(BF16)
 
     pooled_x = x_v[...]
     for j in range(TILES):
@@ -281,8 +298,7 @@
     )
     emb_all[neg] = emb_send[...]
 
-    post(0, 1)
-    serve(1)
+    post_to(STOPS[1], 2)
     loads[2].wait()
     loads[3].wait()
     settle(emb_all.at[pl.ds(0, NEGS - 1)], emb_sem.at[1])
@@ -301,8 +317,7 @@
     )
     sc_all[neg] = scores
 
-    post(1, 0)
-    serve(2)
+    post_to(STOPS[2], 3)
     mates = ask_recv[rep].reshape(NEGS, 128).astype(BF16)
     halves = []
     for h in range(2):
@@ -356,14 +371,7 @@
     )
     eg_recv[neg] = eg_send[neg]
 
-    post(1, 1)
-    lines = (iota((32, 128), 0) == iota((32, 128), 1) + B * (neg % 8)).astype(F32)
-    half = jnp.where(neg // 8 == 0, 0, OWN)
-    mine = tn(loss, lines, HIGH)
-    loss_ref[...] = jnp.sum(
-        jnp.where(iota((128, 128), 0) == half, mine, 0.0), axis=0, keepdims=True
-    )[:, 0:B]
-    cand_out[...] = tn(g_left, e_v[0:32, :])[0:OWN] + tn(g_right, e_v[32:64, :])[OWN:128]
+    post_to(STOPS[3], 4)
     for b in range(8):
         curt_v[b % 2, 128 * (b // 2) : 128 * (b // 2) + 128, :] = (
             cur_v[:, 128 * b : 128 * b + 128].astype(F32).T.astype(BF16)
@@ -378,7 +386,7 @@
         embed_grad.append(nn(move, eg_sum, HIGH))
     embed_grad = jnp.concatenate(embed_grad, axis=1)
 
-    post(2, 0)
+    post_to(STOPS[4])
 
     top_grad = inv_top * embed_grad - top_in * (
         inv_top * inv_top * inv_top * jnp.mean(embed_grad * top_in, axis=1, keepdims=True)
@@ -393,28 +401,27 @@
         total = total + nt(mixed_in_grad[:, j * TILE : (j + 1) * TILE], cw_v[j, F : F + H, :])
     pooled_g[...] = total
 
-    order = (0, 2, 1, 3)
-    for j in order:
+    post_to(STOPS[5])
+
+    def products(j, slot):
         spread_grad = jnp.broadcast_to(
             pooled_g[:, j * TILE : (j + 1) * TILE][:, None, :], (HOP1, SLOTS, TILE)
         ).reshape(REQ, TILE)
-        pgrad_v[...] = jnp.where(mask_v[j].astype(F32) > 0.0, spread_grad * weight, 0.0).astype(
-            BF16
-        )
-        p_send[j] = nn(curt_v[1 - core], pgrad_v[...]).astype(BF16)
+        pgrad_v[slot] = jnp.where(
+            mask_v[j].astype(F32) > 0.0, spread_grad * weight, 0.0
+        ).astype(BF16)
+        p_send[j] = nn(curt_v[1 - core], pgrad_v[slot]).astype(BF16)
         send(p_send.at[j], p_recv.at[j], p_ssem.at[j], p_rsem.at[j], mate)
-        p_own[j] = nn(curt_v[core], pgrad_v[...])
-
-    post(2, 1)
-
-    for j in order:
+        p_own[j] = nn(curt_v[core], pgrad_v[slot])
+
+    def pass_on(j):
         settle(p_recv.at[j], p_rsem.at[j])
         chip_sum = p_own[j] + p_recv[j].astype(F32)
         if j < 2:
             a1_send[j] = chip_sum.astype(BF16).reshape(YS, 128, TILE)
             around(
                 y, YS,
-                lambda q, j=j: send(
+                lambda q: send(
                     a1_send.at[j, q], a1_recv.at[j, y], a1_ssem.at[j], a1_rsem.at[j],
                     (q * CORES + core, neg),
                 ),
@@ -429,11 +436,19 @@
             b1_send[k] = b1_f[...].astype(BF16)
             around(
                 neg, NEGS,
-                lambda n, k=k: send(
+                lambda n: send(
                     b1_send.at[k, n], b1_recv.at[k, neg], b1_ssem.at[k], b1_rsem.at[k], (rep, n)
                 ),
             )
             b1_recv[k, neg] = b1_send[k, neg]
+
+    order = (0, 2, 1, 3)
+    for step, j in enumerate(order):
+        products(j, step % 2)
+        if step > 0:
+            pass_on(order[step - 1])
+    pass_on(order[-1])
+    post_to(STOPS[6])
 
     owner_col = cols_v[:, 0:1]
     rank_col = cols_v[:, 1:2]
@@ -455,10 +470,16 @@
         new = jnp.concatenate([body, tail], axis=1).astype(BF16)
         rows_acc[...] = new if k == 0 else rows_acc[...] + new
 
-    serve(3)
-    post(3, 0)
+    lines = (iota((32, 128), 0) == iota((32, 128), 1) + B * (neg % 8)).astype(F32)
+    half = jnp.where(neg // 8 == 0, 0, OWN)
+    mine = tn(loss, lines, HIGH)
+    loss_ref[...] = jnp.sum(
+        jnp.where(iota((128, 128), 0) == half, mine, 0.0), axis=0, keepdims=True
+    )[:, 0:B]
+    cand_out[...] = tn(g_left, e_v[0:32, :])[0:OWN] + tn(g_right, e_v[32:64, :])[OWN:128]
     place(0)
     place(1)
+    place(2)
 
     for j in range(2):
         settle(a1_recv.at[j, pl.ds(0, YS - 1)], a1_rsem.at[j])
@@ -485,9 +506,9 @@
     )
     b2_recv[y] = b2_send[y]
 
-    post(3, 1)
-    place(2)
+    post_to(STOPS[7])
     place(3)
+
     settle(a2_recv.at[pl.ds(0, NEGS - 1)], a2_sem.at[1])
     a_sum = jnp.sum(a2_recv[...].astype(F32), axis=0)
     settle(b2_recv.at[pl.ds(0, YS - 1)], b2_sem.at[1])
@@ -530,7 +551,7 @@
         pltpu.VMEM((TILES, F + H, TILE), BF16),
         pltpu.VMEM((2 * OWN, H), BF16),
         pltpu.VMEM((TILES, REQ, TILE), BF16),
-        pltpu.VMEM((REQ, TILE), BF16),
+        pltpu.VMEM((2, REQ, TILE), BF16),
         pltpu.VMEM((HOP1, F + H), BF16),
         pltpu.VMEM((HOP1, H), F32),
         pltpu.VMEM((HOP1, H), F32),

time: 98 us -> 93.8 us (0.957)
  Pallas kernels: 93 us -> 89.3 us
    pallas_call x1, Pallas kernels: 93 us -> 89.3 us  [local(): pl.pallas_call(kernel, out_shape=(pltpu.VMEM((REQ, F), BF16), pltpu.VMEM(...]
where the time goes in v6:
time: 93.8 us; the launch traced here: 93.1 us
  Pallas kernels  89.3 us (95%)
  local copies, waits for them, and re-layouts  3.08 us (3%)
    pallas_call x1, Pallas kernels, local(): pl.pallas_call(kernel, out_shape=(pltpu.VMEM((REQ, F), BF16), pltpu.VMEM(...  89.3 us
    unnamed x4, local copies, waits for them, and re-layouts  3.08 us

profile of v6, /device:TPU:0, one launch (start us, length us, event | category | flops | bytes accessed | tf_op | source)
XLA Modules:
  0.0 93.1 jit_solution(6924629150226290070)
XLA Ops:
  0.6 89.3 %step.1 = (bf16[768,1024]{1,0:T(8,128)(2,1)S(1)}, f32[1,4]{1,0:T(1,128)S(1)}, f32[64,2048]{1,0:T(8,128)S(1)}, f32[8,2048]{1,0:T(8,128)S(1)}) custom-call(s32[1,768]{1,0:T(1,128)} %bitcast.5, s32[768]{0:T(1024)} %local_ref.1, s32[16,48]{1,0:T(8,128)} %bitcast.4, s32[4,12]{1,0:T(4,128)} %hop_ref.1, s32[4]{0:T(128)} %pos_ref.1, bf16[1024,1024]{1,0:T(8,128)(2,1)} %table_hbm.1, ...), custom_call_target="tpu_custom_call" | custom-call | tf_op jit(solution)/shard_map/step/pallas_call | solution.py:594
  90.0 1.1 %copy.18 = bf16[768,1024]{1,0:T(8,128)(2,1)} copy(bf16[768,1024]{1,0:T(8,128)(2,1)S(1)} %get-tuple-element.12) | data formatting | bytes 3145728
  91.1 0.5 copy.19
  91.6 0.6 copy.21
  92.3 0.8 copy.20

commit v7 on v6

--- a/solution.py
+++ b/solution.py
@@ -21,7 +21,7 @@
 PART = 256
 WIDE = 3 * PART
 OWN = 64
-STOPS = (16, 26, 38, 50, 58, 64, 64, 64)
+STOPS = (16, 26, 38, 50, 64, 64, 64, 64)
 
 
 def iota(shape, dim):

time: 93.8 us -> 94.9 us (1.012); the launches traced: 93.1 us -> 93.2 us
  no operation moved by 1% of the time
where the time goes in v7:
time: 94.9 us; the launch traced here: 93.2 us
  Pallas kernels  89.5 us (94%)
  local copies, waits for them, and re-layouts  3.08 us (3%)
    pallas_call x1, Pallas kernels, local(): pl.pallas_call(kernel, out_shape=(pltpu.VMEM((REQ, F), BF16), pltpu.VMEM(...  89.5 us
    unnamed x4, local copies, waits for them, and re-layouts  3.08 us

profile of v7, /device:TPU:0, one launch (start us, length us, event | category | flops | bytes accessed | tf_op | source)
XLA Modules:
  0.0 93.2 jit_solution(13882648899137186585)
XLA Ops:
  0.6 89.5 %step.1 = (bf16[768,1024]{1,0:T(8,128)(2,1)S(1)}, f32[1,4]{1,0:T(1,128)S(1)}, f32[64,2048]{1,0:T(8,128)S(1)}, f32[8,2048]{1,0:T(8,128)S(1)}) custom-call(s32[1,768]{1,0:T(1,128)} %bitcast.5, s32[768]{0:T(1024)} %local_ref.1, s32[16,48]{1,0:T(8,128)} %bitcast.4, s32[4,12]{1,0:T(4,128)} %hop_ref.1, s32[4]{0:T(128)} %pos_ref.1, bf16[1024,1024]{1,0:T(8,128)(2,1)} %table_hbm.1, ...), custom_call_target="tpu_custom_call" | custom-call | tf_op jit(solution)/shard_map/step/pallas_call | solution.py:594
  90.1 1.1 %copy.18 = bf16[768,1024]{1,0:T(8,128)(2,1)} copy(bf16[768,1024]{1,0:T(8,128)(2,1)S(1)} %get-tuple-element.12) | data formatting | bytes 3145728
  91.3 0.5 copy.19
  91.8 0.6 copy.21
  92.4 0.8 copy.20
